TPU v7x, 32 devices: a whole 2x2x4 slice. The times are simulated.
32 devices in a mesh: dp: 16 (over z, x, core), tensor: 2 (over y).
Axes of the slice: x: 2, y: 2, z: 4, core: 2. Of those that a mesh axis runs over, the one named last changes fastest.
Arguments:
- tokens: bfloat16 [18912, 768], P(('dp', 'tensor')), may hold values from -6 to 6
- patch_mask: int32 [18912], P(('dp', 'tensor')), may hold values from 0 to 1, as said below
- mask_token: float32 [768], replicated, may hold values from -5 to 5
- norm1_gain: float32 [768], replicated, may hold values from 0.1 to 1.9
- norm1_shift: float32 [768], replicated, may hold values from -3 to 3
- w_qkv: bfloat16 [3, 768, 768], P(None, None, 'tensor'), may hold values from -0.21875 to 0.21875
- qv_bias: float32 [2, 768], P(None, 'tensor'), may hold values from -3 to 3
- w_proj: bfloat16 [768, 768], P('tensor'), may hold values from -0.875 to 0.875
- proj_bias: float32 [768], replicated, may hold values from -3 to 3
- layer_scales: float32 [2, 768], replicated, may hold values from 0.5 to 1.5
- norm2_gain: float32 [768], replicated, may hold values from 0.1 to 1.9
- norm2_shift: float32 [768], replicated, may hold values from -3 to 3
- w_up: bfloat16 [768, 3072], P(None, 'tensor'), may hold values from -0.21875 to 0.21875
- up_bias: float32 [3072], P('tensor'), may hold values from -3 to 3
- w_down: bfloat16 [3072, 768], P('tensor'), may hold values from -0.109375 to 0.109375
- down_bias: float32 [768], replicated, may hold values from -3 to 3
- cotangent: bfloat16 [18912, 768], P(('dp', 'tensor')), may hold values from -6 to 6
Outputs:
- output: bfloat16 [18912, 768], P(('dp', 'tensor'))
- grad_tokens: bfloat16 [18912, 768], P(('dp', 'tensor'))
- grad_mask_token: float32 [768], replicated
- grad_norm1_gain: float32 [768], replicated
- grad_norm1_shift: float32 [768], replicated
- grad_w_qkv: float32 [3, 768, 768], P(None, None, 'tensor')
- grad_qv_bias: float32 [2, 768], P(None, 'tensor')
- grad_w_proj: float32 [768, 768], P('tensor')
- grad_proj_bias: float32 [768], replicated
- grad_layer_scales: float32 [2, 768], replicated
- grad_norm2_gain: float32 [768], replicated
- grad_norm2_shift: float32 [768], replicated
- grad_w_up: float32 [768, 3072], P(None, 'tensor')
- grad_up_bias: float32 [3072], P('tensor')
- grad_w_down: float32 [3072, 768], P('tensor')
- grad_down_bias: float32 [768], replicated
Inputs may be any that keep to these rules, and one draw needn't show every extreme that they name: `patch_mask`: row 0 of each image (its class row) is 0; of the other 196 rows of an image, between (392) // 5 + 1 and (784) // 5 are 1.
All inputs are finite; a program needn't handle non-finite values.
Results may differ from a plain program's by a relative error of at most 0.017.
Values may be sent and summed in bfloat16 or wider, within the bound.
A program may use at most 192 MiB of HBM per device.

v0:
```python
import jax
import jax.numpy as jnp
from jax import lax
from jax.sharding import PartitionSpec as P

HD = 64
L = 197


EPS = 1e-06
INV_ROOT2 = 0.7071067811865476
INV_ROOT2PI = 0.3989422804014327


def norm_stats(rows):
    row_mean = jnp.mean(rows, axis=-1, keepdims=True)
    centred = rows - row_mean
    inverse = lax.rsqrt(jnp.mean(centred * centred, axis=-1, keepdims=True) + EPS)
    return (centred * inverse, inverse)


def norm_back(grad_normed, gain, scaled, inverse):
    weighted = grad_normed * gain
    inner = (
        weighted
        - jnp.mean(weighted, axis=-1, keepdims=True)
        - scaled * jnp.mean(weighted * scaled, axis=-1, keepdims=True)
    )
    return (inverse * inner, jnp.sum(grad_normed * scaled, axis=0), jnp.sum(grad_normed, axis=0))


def gelu_exact(values_in):
    return 0.5 * values_in * (1.0 + lax.erf(values_in * INV_ROOT2))


def gelu_slope(values_in):
    return (
        0.5 * (1.0 + lax.erf(values_in * INV_ROOT2))
        + values_in * jnp.exp(-0.5 * values_in * values_in) * INV_ROOT2PI
    )


def split_heads(matrix):
    return matrix.reshape(matrix.shape[0] // L, L, matrix.shape[1] // HD, HD)


def local(
    tokens,
    patch_mask,
    mask_token,
    norm1_gain,
    norm1_shift,
    w_qkv,
    qv_bias,
    w_proj,
    proj_bias,
    layer_scales,
    norm2_gain,
    norm2_shift,
    w_up,
    up_bias,
    w_down,
    down_bias,
    cotangent,
):
    masked = (patch_mask == 1)[:, None]
    mixed = jnp.where(masked, mask_token[None, :], tokens.astype(jnp.float32))
    scaled1, inverse1 = norm_stats(mixed)
    normed1 = (scaled1 * norm1_gain + norm1_shift).astype(jnp.bfloat16)
    normed1_all = lax.all_gather(normed1, "tensor", axis=0, tiled=True)
    project = jnp.einsum("rd,pde->pre", normed1_all, w_qkv, preferred_element_type=jnp.float32)
    queries = ((project[0] + qv_bias[0]) * 0.125).astype(jnp.bfloat16)
    keys_all = project[1].astype(jnp.bfloat16)
    values = (project[2] + qv_bias[1]).astype(jnp.bfloat16)
    query_heads = split_heads(queries)
    key_heads = split_heads(keys_all)
    value_heads = split_heads(values)
    scores = jnp.einsum(
        "bqhe,bkhe->bhqk", query_heads, key_heads, preferred_element_type=jnp.float32
    )
    top_score = jnp.max(scores, axis=-1, keepdims=True)
    exponent = jnp.exp(scores - top_score)
    totals = jnp.sum(exponent, axis=-1, keepdims=True)
    log_total = top_score + jnp.log(totals)
    probs_low = (exponent / totals).astype(jnp.bfloat16)
    heads_mix = jnp.einsum(
        "bhqk,bkhe->bqhe", probs_low, value_heads, preferred_element_type=jnp.float32
    )
    heads_out = heads_mix.reshape(queries.shape).astype(jnp.bfloat16)
    piece = heads_out
    branch1 = (
        lax.psum_scatter(
            jnp.dot(piece, w_proj, preferred_element_type=jnp.float32).astype(jnp.bfloat16),
            "tensor",
            scatter_dimension=0,
            tiled=True,
        ).astype(jnp.float32)
        + proj_bias
    )
    middle = mixed + layer_scales[0] * branch1
    scaled2, inverse2 = norm_stats(middle)
    normed2 = (scaled2 * norm2_gain + norm2_shift).astype(jnp.bfloat16)
    normed2_all = lax.all_gather(normed2, "tensor", axis=0, tiled=True)
    hidden_pre = jnp.dot(normed2_all, w_up, preferred_element_type=jnp.float32) + up_bias
    hidden_act = gelu_exact(hidden_pre).astype(jnp.bfloat16)
    piece = hidden_act
    branch2 = (
        lax.psum_scatter(
            jnp.dot(piece, w_down, preferred_element_type=jnp.float32).astype(jnp.bfloat16),
            "tensor",
            scatter_dimension=0,
            tiled=True,
        ).astype(jnp.float32)
        + down_bias
    )
    output = (middle + layer_scales[1] * branch2).astype(jnp.bfloat16)
    grad_out = cotangent.astype(jnp.float32) * masked.astype(jnp.float32)
    grad_scale2 = jnp.sum(grad_out * branch2, axis=0)
    grad_branch2 = (layer_scales[1] * grad_out).astype(jnp.bfloat16)
    grad_down_bias = jnp.sum(grad_branch2.astype(jnp.float32), axis=0)
    grad_branch2_all = lax.all_gather(grad_branch2, "tensor", axis=0, tiled=True)
    grad_w_down = jnp.einsum(
        "rf,rd->fd", hidden_act, grad_branch2_all, preferred_element_type=jnp.float32
    )
    grad_act = jnp.einsum("rd,fd->rf", grad_branch2_all, w_down, preferred_element_type=jnp.float32)
    grad_pre = (grad_act * gelu_slope(hidden_pre)).astype(jnp.bfloat16)
    grad_up_bias = jnp.sum(grad_pre.astype(jnp.float32), axis=0)
    grad_w_up = jnp.einsum("rd,rf->df", normed2_all, grad_pre, preferred_element_type=jnp.float32)
    piece = grad_pre
    grad_normed2 = lax.psum_scatter(
        jnp.einsum("rf,df->rd", piece, w_up, preferred_element_type=jnp.float32).astype(
            jnp.bfloat16
        ),
        "tensor",
        scatter_dimension=0,
        tiled=True,
    ).astype(jnp.float32)
    grad_into2, grad_norm2_gain, grad_norm2_shift = norm_back(
        grad_normed2, norm2_gain, scaled2, inverse2
    )
    grad_middle = grad_out + grad_into2
    grad_scale1 = jnp.sum(grad_middle * branch1, axis=0)
    grad_branch1 = (layer_scales[0] * grad_middle).astype(jnp.bfloat16)
    grad_proj_bias = jnp.sum(grad_branch1.astype(jnp.float32), axis=0)
    grad_branch1_all = lax.all_gather(grad_branch1, "tensor", axis=0, tiled=True)
    grad_w_proj = jnp.einsum(
        "re,rd->ed", heads_out, grad_branch1_all, preferred_element_type=jnp.float32
    )
    grad_heads = jnp.einsum(
        "rd,ed->re", grad_branch1_all, w_proj, preferred_element_type=jnp.float32
    ).astype(jnp.bfloat16)
    grad_head_split = split_heads(grad_heads)
    scores_again = jnp.einsum(
        "bqhe,bkhe->bhqk", query_heads, key_heads, preferred_element_type=jnp.float32
    )
    probs = jnp.exp(scores_again - log_total)
    grad_probs = jnp.einsum(
        "bqhe,bkhe->bhqk", grad_head_split, value_heads, preferred_element_type=jnp.float32
    )
    grad_scores = (
        probs * (grad_probs - jnp.sum(grad_probs * probs, axis=-1, keepdims=True))
    ).astype(jnp.bfloat16)
    grad_queries = (
        (
            jnp.einsum(
                "bhqk,bkhe->bqhe", grad_scores, key_heads, preferred_element_type=jnp.float32
            )
            * 0.125
        )
        .reshape(queries.shape)
        .astype(jnp.bfloat16)
    )
    grad_keys = (
        jnp.einsum("bhqk,bqhe->bkhe", grad_scores, query_heads, preferred_element_type=jnp.float32)
        .reshape(queries.shape)
        .astype(jnp.bfloat16)
    )
    grad_values = (
        jnp.einsum(
            "bhqk,bqhe->bkhe", probs_low, grad_head_split, preferred_element_type=jnp.float32
        )
        .reshape(queries.shape)
        .astype(jnp.bfloat16)
    )
    stacked = jnp.stack([grad_queries, grad_keys, grad_values])
    grad_w_qkv = jnp.einsum("rd,pre->pde", normed1_all, stacked, preferred_element_type=jnp.float32)
    grad_qv_bias = jnp.stack(
        [
            jnp.sum(grad_queries.astype(jnp.float32), axis=0),
            jnp.sum(grad_values.astype(jnp.float32), axis=0),
        ]
    )
    piece = stacked
    grad_normed1 = lax.psum_scatter(
        jnp.einsum("pre,pde->rd", piece, w_qkv, preferred_element_type=jnp.float32).astype(
            jnp.bfloat16
        ),
        "tensor",
        scatter_dimension=0,
        tiled=True,
    ).astype(jnp.float32)
    grad_into1, grad_norm1_gain, grad_norm1_shift = norm_back(
        grad_normed1, norm1_gain, scaled1, inverse1
    )
    grad_mixed = grad_middle + grad_into1
    grad_tokens = jnp.where(masked, 0.0, grad_mixed).astype(jnp.bfloat16)
    grad_mask_token = jnp.sum(jnp.where(masked, grad_mixed, 0.0), axis=0)
    grad_w_qkv, grad_qv_bias, grad_w_proj, grad_w_up, grad_up_bias, grad_w_down = lax.psum(
        (grad_w_qkv, grad_qv_bias, grad_w_proj, grad_w_up, grad_up_bias, grad_w_down), "dp"
    )
    grad_layer_scales = jnp.stack([grad_scale1, grad_scale2])
    (
        grad_mask_token,
        grad_norm1_gain,
        grad_norm1_shift,
        grad_proj_bias,
        grad_layer_scales,
        grad_norm2_gain,
        grad_norm2_shift,
        grad_down_bias,
    ) = lax.psum(
        (
            grad_mask_token,
            grad_norm1_gain,
            grad_norm1_shift,
            grad_proj_bias,
            grad_layer_scales,
            grad_norm2_gain,
            grad_norm2_shift,
            grad_down_bias,
        ),
        ("dp", "tensor"),
    )
    return (
        output,
        grad_tokens,
        grad_mask_token,
        grad_norm1_gain,
        grad_norm1_shift,
        grad_w_qkv,
        grad_qv_bias,
        grad_w_proj,
        grad_proj_bias,
        grad_layer_scales,
        grad_norm2_gain,
        grad_norm2_shift,
        grad_w_up,
        grad_up_bias,
        grad_w_down,
        grad_down_bias,
    )


def solution(mesh):
    return jax.shard_map(
        local,
        mesh=mesh,
        in_specs=(
            P(("dp", "tensor"), None),
            P(("dp", "tensor")),
            P(),
            P(),
            P(),
            P(None, None, "tensor"),
            P(None, "tensor"),
            P("tensor", None),
            P(),
            P(),
            P(),
            P(),
            P(None, "tensor"),
            P("tensor"),
            P("tensor", None),
            P(),
            P(("dp", "tensor"), None),
        ),
        out_specs=(
            P(("dp", "tensor"), None),
            P(("dp", "tensor"), None),
            P(),
            P(),
            P(),
            P(None, None, "tensor"),
            P(None, "tensor"),
            P("tensor", None),
            P(),
            P(),
            P(),
            P(),
            P(None, "tensor"),
            P("tensor"),
            P("tensor", None),
            P(),
        ),
        check_vma=False,
    )
```

profile of v0, /device:TPU:0, one launch (start us, length us, event | category | flops | bytes accessed | tf_op | source)
XLA Modules:
  0.0 622.5 jit_solution(11330366483130989605)
XLA Ops:
  16.1 30.1 %all-gather.9.cloned.1.call-done = bf16[2,591,768]{2,1,0:T(8,128)(2,1)} async-done(((bf16[1,591,768]{2,1,0:T(8,128)(2,1)}), bf16[2,591,768]{2,1,0:T(8,128)(2,1)}) %all-gather.9.cloned.1.call-update) | async-done | bytes 1815568 | tf_op jit(solution)/shard_map/all_gather | solution.py:70
  100.1 25.9 %fusion = bf16[592,768]{1,0:T(8,128)(2,1)} fusion(bf16[1182,768]{1,0:T(8,128)(2,1)} %convolution_convert_fusion), kind=kCustom, calls=%all-reduce-scatter | all-reduce-scatter fusion | flops 909313 | bytes 2725376
  131.6 6.4 %concatenate = bf16[593,768]{1,0:T(8,128)(2,1)} concatenate(bf16[1,768]{1,0:T(2,128)(2,1)S(1)} %collective-permute-done, bf16[592,768]{1,0:T(8,128)(2,1)} %fusion), dimensions={0} | concatenate | bytes 1821696
  146.1 28.7 %all-gather.11.cloned.1.call-done = bf16[2,591,768]{2,1,0:T(8,128)(2,1)} async-done(((bf16[1,591,768]{2,1,0:T(8,128)(2,1)}), bf16[2,591,768]{2,1,0:T(8,128)(2,1)}) %all-gather.11.cloned.1.call-update) | async-done | bytes 1815568 | tf_op jit(solution)/shard_map/all_gather | solution.py:103
  177.8 6.0 multiply_convert_fusion.1
  183.9 5.5 convert_reduce_fusion
  195.3 25.2 %fusion.2 = bf16[592,768]{1,0:T(8,128)(2,1)S(1)} fusion(bf16[1182,768]{1,0:T(8,128)(2,1)} %convolution_convert_fusion.1), kind=kCustom, calls=%all-reduce-scatter.2 | all-reduce-scatter fusion | flops 909313 | bytes 2725376
  225.3 5.1 concatenate.2
  238.2 8.2 %fusion.50 = f32[768,1536]{1,0:T(8,128)} fusion(bf16[1182,768]{1,0:T(8,128)(2,1)} %reshape.160, bf16[1182,1536]{1,0:T(8,128)(2,1)} %copy-done.44), kind=kOutput, calls=%fused_computation.114 | convolution fusion | flops 2788687872 | bytes 10165248 | tf_op jit(solution)/shard_map/rd,rf->df/dot_general | solution.py:128
  246.3 5.1 fusion.51
  251.4 18.5 %all-gather.15.cloned.1.call-done = bf16[2,591,768]{2,1,0:T(8,128)(2,1)} async-done(((bf16[1,591,768]{2,1,0:T(8,128)(2,1)}), bf16[2,591,768]{2,1,0:T(8,128)(2,1)}) %all-gather.15.cloned.1.call-update) | async-done | bytes 1815568 | tf_op jit(solution)/shard_map/all_gather | solution.py:145
  288.1 8.1 %multiply_reduce_fusion = (f32[6,6,197]{2,1,0:T(8,128)S(1)}, f32[6,6,197,197]{2,3,1,0:T(8,128)}) fusion(f32[6,6,197,197]{2,3,1,0:T(8,128)} %copy-done.2, f32[6,6,197]{2,1,0:T(8,128)S(1)} %log_add_fusion, bf16[6,197,6,64]{1,3,2,0:T(8,128)(2,1)S(1)} %copy.77, bf16[6,197,6,64]{1,0,3,2:T(8,128)(2,1)S(1)} %copy-done.14), kind=kOutput, calls=%fused_computation.5 | convolution fusion | flops 183016144 | bytes 13049280 | tf_op jit(solution)/shard_map/bqhe,bkhe->bhqk/dot_general | solution.py:157
  296.1 6.7 %multiply_convert_fusion = bf16[6,6,197,197]{2,3,1,0:T(8,128)(2,1)} fusion(f32[6,6,197,197]{2,3,1,0:T(8,128)} %get-tuple-element.113, f32[6,6,197,197]{2,3,1,0:T(8,128)S(1)} %bitcast.71, f32[6,6,197]{2,1,0:T(8,128)S(1)} %get-tuple-element.112, f32[6,6,197]{2,1,0:T(8,128)S(1)} %log_add_fusion), kind=kLoop, calls=%fused_computation.4 | loop fusion | flops 5588496 | bytes 14027976 | tf_op jit(solution)/shard_map/convert_element_type | solution.py:162
  302.8 5.1 fusion.31
  339.9 7.0 %convolution_convert_fusion.2 = bf16[1182,768]{1,0:T(8,128)(2,1)} fusion(bf16[1182,1536]{1,0:T(8,128)(2,1)} %get-tuple-element.110, bf16[1536,768]{1,0:T(8,128)(2,1)} %param.31), kind=kOutput, calls=%fused_computation.22 | convolution fusion | flops 2789595648 | bytes 7805952 | tf_op jit(solution)/shard_map/dot_general | solution.py:109
  347.1 6.1 fusion.10
  353.2 46.0 %fusion.43 = (bf16[592,768]{1,0:T(8,128)(2,1)S(1)}, bf16[592,768]{1,0:T(8,128)(2,1)}) fusion(bf16[1182,768]{1,0:T(8,128)(2,1)} %convolution_convert_fusion.2, bf16[1182,768]{1,0:T(8,128)(2,1)} %fusion.10), kind=kCustom, calls=%all-reduce-scatter.4 | all-reduce-scatter fusion | flops 1818625 | bytes 5450240
  403.9 63.8 %all-reduce.9 = (f32[2,384]{1,0:T(2,128)}, f32[1536]{0:T(1024)}) all-reduce(f32[2,384]{1,0:T(2,128)S(1)} %pad_maximum_fusion.1, f32[1536]{0:T(1024)S(1)} %get-tuple-element.118), channel_id=1, replica_groups=mesh['dp'=16,'tensor'=2] {'dp'}, use_global_device_ids=true, to_apply=%region_24.25 | all-reduce | flops 2304 | bytes 18432 | tf_op jit(solution)/shard_map/psum | solution.py:208
  467.7 6.1 concatenate.3
  473.8 6.1 concatenate.1
  487.4 38.8 %all-reduce.8 = (f32[768]{0:T(1024)}, f32[768]{0:T(1024)}, f32[768]{0:T(1024)}, f32[768]{0:T(1024)}, f32[2,768]{1,0:T(2,128)}, /*index=5*/f32[768]{0:T(1024)}, f32[768]{0:T(1024)}, f32[768]{0:T(1024)}) all-reduce(f32[768]{0:T(1024)S(1)} %get-tuple-element.106, ...), channel_id=1, replica_groups=mesh['dp'=16,'tensor'=2] {'dp','tensor'}, use_global_device_ids=true, to_apply=%region_16.17 | all-reduce | flops 6912 | bytes 55296 | tf_op jit(solution)/shard_map/psum | solution.py:221
  528.6 71.9 %all-reduce.14.cloned.1.call-done = (f32[3,768,384]{1,2,0:T(8,128)}, f32[384,768]{1,0:T(8,128)}, f32[768,1536]{1,0:T(8,128)}, f32[1536,768]{1,0:T(8,128)}) async-done(((f32[3,768,384]{1,2,0:T(8,128)}, f32[384,768]{1,0:T(8,128)}, f32[768,1536]{1,0:T(8,128)}, f32[1536,768]{1,0:T(8,128)}), (f32[3,768,384]{1,2,0:T(8,128)}, f32[384,768]{1,0:T(8,128)}, f32[768,1536]{1,0:T(8,128)}, ...) | async-done | bytes 14155792 | tf_op jit(solution)/shard_map/psum | solution.py:208
  600.5 5.2 copy.91
  606.8 5.5 copy.125
  (199 shorter events, 166.2 us)
Async XLA Ops:
  7.2 170.7 %copy-start = (bf16[768,1536]{1,0:T(8,128)(2,1)S(1)}, bf16[768,1536]{1,0:T(8,128)(2,1)}, u32[]{:S(2)}) copy-start(bf16[768,1536]{1,0:T(8,128)(2,1)} %param.29) | copy-start | bytes 7077892
  7.2 39.0 %all-gather.9.cloned.1.call-start = ((), (), s32[]{:S(2)}) async-start(), calls=%async_computation | async-start | bytes 2727936 | tf_op jit(solution)/shard_map/all_gather | solution.py:70
  13.4 129.6 %all-gather.13.cloned.1.call-start = ((), (), s32[]{:S(2)}) async-start(), calls=%async_computation.2 | async-start | bytes 2727936 | tf_op jit(solution)/shard_map/all_gather | solution.py:121
  15.9 158.9 %all-gather.11.cloned.1.call-start = ((), (), s32[]{:S(2)}) async-start(), calls=%async_computation.1 | async-start | bytes 2727936 | tf_op jit(solution)/shard_map/all_gather | solution.py:103
  100.1 30.1 %copy-start.40 = (u32[32]{0:T(128)S(1)}, u32[32]{0:T(128)}, u32[]{:S(2)}) copy-start(u32[32]{0:T(128)} %constant.36) | copy-start | bytes 388
  100.1 37.9 %copy-start.32 = (f32[768]{0:T(1024)S(1)}, f32[768]{0:T(1024)}, u32[]{:S(2)}) copy-start(f32[768]{0:T(1024)} %param.25) | copy-start | bytes 9220
  126.8 4.8 collective-permute-start
  142.9 127.0 %all-gather.15.cloned.1.call-start = ((), (), s32[]{:S(2)}) async-start(), calls=%async_computation.3 | async-start | bytes 2727936 | tf_op jit(solution)/shard_map/all_gather | solution.py:145
  146.1 31.8 %copy-start.43 = (f32[1536]{0:T(1024)S(1)}, f32[1536]{0:T(1024)}, u32[]{:S(2)}) copy-start(f32[1536]{0:T(1024)} %param.30) | copy-start | bytes 18436
  177.8 6.0 copy-start.41
  195.3 35.1 %copy-start.6 = (bf16[593,768]{1,0:T(8,128)(2,1)S(1)}, bf16[593,768]{1,0:T(8,128)(2,1)}, u32[]{:S(2)}) copy-start(bf16[593,768]{1,0:T(8,128)(2,1)} %concatenate) | copy-start | bytes 2732548
  220.6 4.8 collective-permute-start.2
  238.1 362.4 %all-reduce.14.cloned.1.call-start = ((), (), s32[]{:S(2)}) async-start(), calls=%async_computation.4 | async-start | bytes 28311552 | tf_op jit(solution)/shard_map/psum | solution.py:208
  238.1 8.2 %copy-start.26 = (bf16[1182,768]{1,0:T(8,128)(2,1)S(1)}, bf16[1182,768]{1,0:T(8,128)(2,1)}, u32[]{:S(2)}) copy-start(bf16[1182,768]{1,0:T(8,128)(2,1)} %reshape.162) | copy-start | bytes 5446660
  238.2 8.2 %copy-start.45 = (bf16[1182,1536]{1,0:T(8,128)(2,1)S(1)}, bf16[1182,1536]{1,0:T(8,128)(2,1)}, u32[]{:S(2)}) copy-start(bf16[1182,1536]{1,0:T(8,128)(2,1)} %get-tuple-element.110) | copy-start | bytes 10893316
  251.4 21.6 %copy-start.29 = (bf16[1182,384]{0,1:T(8,128)(2,1)S(1)}, bf16[1182,384]{0,1:T(8,128)(2,1)}, u32[]{:S(2)}) copy-start(bf16[1182,384]{0,1:T(8,128)(2,1)} %convert_element_type.168) | copy-start | bytes 2723332
  283.5 12.6 %slice-start = ((s8[7372800]{0:T(1024)(128)(4,1)}), s8[4194304]{0:T(1024)(128)(4,1)S(1)}, s32[]{:S(2)}) async-start(s8[7372800]{0:T(1024)(128)(4,1)} %bitcast.70), calls=%async_computation.5 | async-start | bytes 8388608
  288.1 8.1 %slice-start.1 = ((s8[7372800]{0:T(1024)(128)(4,1)}), s8[3178496]{0:T(1024)(128)(4,1)S(1)}, s32[]{:S(2)}) async-start(s8[7372800]{0:T(1024)(128)(4,1)} %bitcast.70), calls=%async_computation.6 | async-start | bytes 6356992
  399.2 68.5 %copy-start.21 = (bf16[592,768]{1,0:T(8,128)(2,1)}, bf16[592,768]{1,0:T(8,128)(2,1)S(1)}, u32[]{:S(2)}) copy-start(bf16[592,768]{1,0:T(8,128)(2,1)S(1)} %get-tuple-element.96) | copy-start | bytes 2727940
  399.9 67.7 %collective-permute-start.3 = (bf16[1,768]{1,0:T(2,128)(2,1)S(1)}, bf16[1,768]{1,0:T(2,128)(2,1)S(1)}, u32[]{:S(2)}, u32[]{:S(2)}) collective-permute-start(bf16[1,768]{1,0:T(2,128)(2,1)S(1)} %slice.37), channel_id=1, source_target_pairs={{0,1},{2,3},{4,5},{6,7},{8,9},{10,11},{12,13},{14,15},{16,17},{18,... | collective-permute-start | bytes 4616
  402.6 71.2 %collective-permute-start.1 = (bf16[1,768]{1,0:T(2,128)(2,1)S(1)}, bf16[1,768]{1,0:T(2,128)(2,1)S(1)}, u32[]{:S(2)}, u32[]{:S(2)}) collective-permute-start(bf16[1,768]{1,0:T(2,128)(2,1)S(1)} %slice.35), channel_id=1, source_target_pairs={{0,1},{2,3},{4,5},{6,7},{8,9},{10,11},{12,13},{14,15},{16,17},{18,... | collective-permute-start | bytes 4616
  473.8 8.7 %copy-start.18 = (bf16[591,768]{1,0:T(8,128)(2,1)S(1)}, bf16[591,768]{1,0:T(8,128)(2,1)}, u32[]{:S(2)}) copy-start(bf16[591,768]{1,0:T(8,128)(2,1)} %param.33) | copy-start | bytes 2723332
  473.8 8.7 %copy-start.38 = (f32[768]{0:T(1024)S(1)}, f32[768]{0:T(1024)}, u32[]{:S(2)}) copy-start(f32[768]{0:T(1024)} %param.32) | copy-start | bytes 9220
  605.8 6.5 %slice-start.2 = ((s8[4718592]{0:T(1024)(128)(4,1)}), s8[4194304]{0:T(1024)(128)(4,1)S(1)}, s32[]{:S(2)}) async-start(s8[4718592]{0:T(1024)(128)(4,1)} %bitcast.73), calls=%async_computation.7 | async-start | bytes 8388608
  (35 other events, 112.5 us)
Sparse Core Ops, SparseCore 0:
  13.5 32.6 all-gather.8
  48.4 29.9 all-gather.12
  143.0 31.6 all-gather.10
  238.2 31.6 all-gather.14
  340.0 260.4 all-reduce.13
where the time goes:
time: 629 us; the launch traced here: 622 us
  blocking collectives  200 us (32%)
  waiting for transfers between devices  151 us (24%)
  local copies, waits for them, and re-layouts  123 us (20%)
  matrix products  80.9 us (13%)
  other arithmetic  42.2 us (7%)
  between operations  15.3 us (2%)
  starting transfers between devices  11.1 us (2%)
    unnamed x3, blocking collectives  97.1 us
    psum x1, waiting for transfers between devices, local(): lax.psum((grad_w_qkv, grad_qv_bias, grad_w_proj, grad_w_up, grad_up_bias,...  71.9 us
    psum x1, blocking collectives, local(): lax.psum((grad_w_qkv, grad_qv_bias, grad_w_proj, grad_w_up, grad_up_bias,...  63.8 us
    unnamed x119, local copies, waits for them, and re-layouts  63.3 us
    psum x1, blocking collectives, local(): lax.psum((grad_mask_token, grad_norm1_gain, grad_norm1_shift, grad_proj_b...  38.8 us
    all_gather x1, waiting for transfers between devices, local(): normed1_all = lax.all_gather(normed1, 'tensor', axis=0, tiled=True)  30.1 us
    all_gather x1, waiting for transfers between devices, local(): normed2_all = lax.all_gather(normed2, 'tensor', axis=0, tiled=True)  28.7 us
    all_gather x1, waiting for transfers between devices, local(): lax.all_gather(grad_branch1, 'tensor', axis=0, tiled=True)  18.5 us
  transfers between devices with their start and end apart: 9, of which 6 were waited for; matrix products, arithmetic and copies ran while one was open for 30% of the time, Pallas kernels for 0%

commit v1 on v0

v1 whole, which is shorter than its diff:
```python
import functools

import jax
import jax.numpy as jnp
from jax import lax
from jax.experimental import pallas as pl
from jax.experimental.pallas import tpu as pltpu
from jax.sharding import PartitionSpec as P

MESH = pl.DeviceIdType.MESH
F32 = jnp.float32
BF16 = jnp.bfloat16
L = 197
LP = 208
D = 768
EPS = 1e-06
INV_ROOT2 = 0.7071067811865476
INV_ROOT2PI = 0.3989422804014327

MTOK, N1G, N1S, PB, LS0, LS1, N2G, N2S, DB, QVO, UPO, QVX, UPX = (
    0, 1, 2, 3, 4, 5, 6, 7, 8, 9, 10, 12, 13)
NSUM = 9
NVEC = 16


def dot(a, b):
    return lax.dot_general(a, b, (((1,), (0,)), ((), ())), preferred_element_type=F32)


def dot_nt(a, b):
    return lax.dot_general(a, b, (((1,), (1,)), ((), ())), preferred_element_type=F32)


def fold(x):
    return jnp.sum(x.reshape(x.shape[0] // 8, 8, x.shape[1]), axis=0)


def normed(rows):
    centred = rows - jnp.mean(rows, axis=-1, keepdims=True)
    inverse = lax.rsqrt(jnp.mean(centred * centred, axis=-1, keepdims=True) + EPS)
    return centred * inverse, inverse


def norm_back(grad, gain, scaled, inverse):
    weighted = grad * gain
    inner = (
        weighted
        - jnp.mean(weighted, axis=-1, keepdims=True)
        - scaled * jnp.mean(weighted * scaled, axis=-1, keepdims=True)
    )
    return inverse * inner


def wide(column):
    return jnp.concatenate([column] * (D // 128), axis=1)


BLOCKS = ((0, 48), (48, 48), (96, 48), (144, 48), (192, 16))


VECTORS = ("mtok", "n1g", "n1s", "pb", "n2g", "n2s", "db")


class Layer:
    def __init__(self, r, rows):
        self.__dict__.update(r)
        self.rows = rows
        self.images = rows // L
        self.padded = self.images * LP

    def widen(self, src):
        n = self.rows // 16

        @pl.loop(0, n)
        def _(b):
            at = pl.ds(pl.multiple_of(b * 16, 16), 16)
            self.t32[at, :] = src[at, :].astype(F32)

        left = self.rows - n * 16
        if left:
            self.t32[n * 16 : self.rows, :] = src[n * 16 : self.rows, :].astype(F32)

    def narrow(self, src, dst):
        for i in range(self.images):
            for r, n in BLOCKS:
                n = min(n, L - r)
                self.t32[pl.ds(L * i + r, n), :] = src[pl.ds(LP * i + r, n), :].astype(F32)
        n = self.rows // 16

        @pl.loop(0, n)
        def _(b):
            at = pl.ds(pl.multiple_of(b * 16, 16), 16)
            dst[at, :] = self.t32[at, :].astype(BF16)

        left = self.rows - n * 16
        if left:
            dst[n * 16 : self.rows, :] = self.t32[n * 16 : self.rows, :].astype(BF16)

    def row_loop(self, body):
        @pl.loop(0, self.padded // 48)
        def _(b):
            body(pl.ds(pl.multiple_of(b * 48, 48), 48))

    def acc(self, at, x):
        self.vacc[pl.ds(at * 8, 8), :] += fold(x)

    def vectors(self):
        for name in ("mtok", "n1g", "n1s", "pb", "n2g", "n2s", "db"):
            self.__dict__[name] = self.rows8.at[pl.ds(VECTORS.index(name), 1), :]
            self.rows8[VECTORS.index(name), :] = self.__dict__["in_" + name][...]

    def start(self):
        self.vacc[...] = jnp.zeros_like(self.vacc)
        rows = self.rows
        self.mrow[...] = jnp.zeros_like(self.mrow)
        flags = jnp.where(self.mask[...] == 1, 1.0, 0.0).astype(F32)[None, :]
        self.mrow[:, pl.ds(0, rows)] = jnp.broadcast_to(flags, (128, rows))
        self.mcol[...] = jnp.transpose(self.mrow[...])
        self.t32[pl.ds(rows, self.t32.shape[0] - rows), :] = jnp.zeros(
            (self.t32.shape[0] - rows, D), F32)
        self.widen(self.tok)
        for i in range(self.images):
            for r, n in BLOCKS:
                at = pl.ds(L * i + r, n)
                to = pl.ds(LP * i + r, n)
                x = self.t32[at, :]
                mk = self.mcol[at, :]
                mx = jnp.where(wide(mk) > 0.5, self.mtok[...], x)
                if r + n > L:
                    keep = lax.broadcasted_iota(jnp.int32, (n, 128), 0) < L - r
                    mk = jnp.where(keep, mk, 0.0)
                    mx = jnp.where(wide(keep), mx, 0.0)
                self.maskp[to, :] = mk
                self.mixed[to, :] = mx
                sc, _ = normed(mx)
                self.n1[to, :] = (sc * self.n1g[...] + self.n1s[...]).astype(BF16)

    def start2(self):
        self.n1t[...] = jnp.transpose(self.n1[...])
        self.widen(self.cot)
        for i in range(self.images):
            for r, n in BLOCKS:
                at = pl.ds(L * i + r, n)
                to = pl.ds(LP * i + r, n)
                go = self.t32[at, :] * wide(self.maskp[to, :])
                self.gout[to, :] = go.astype(BF16)
                self.gb[to, :] = (self.ls[1:2, :] * go).astype(BF16)

    def w_pair(self, j, h):
        return jnp.concatenate(
            [self.g_at[j, h, pl.ds(p * D, D), :] for p in range(3)], axis=1)

    def qkv(self, j, h):
        t = h * 3 + j
        proj = dot(self.n1[...], self.w_pair(j, h))
        qb = self.qb[pl.ds(t, 1), :]
        vb = self.qb[pl.ds(8 + t, 1), :]
        self.q[t] = ((proj[:, 0:128] + qb) * 0.125).astype(BF16)
        self.k[t] = proj[:, 128:256].astype(BF16)
        self.v[t] = (proj[:, 256:384] + vb).astype(BF16)

    def two(self, x):
        low = lax.broadcasted_iota(jnp.int32, x.shape, 1) < 64
        zero = jnp.zeros_like(x)
        return jnp.where(low, x, zero), jnp.where(low, zero, x)

    def attend(self, t):
        for i in range(self.images):
            at = pl.ds(i * LP, LP)
            q0, q1 = self.two(self.q[t, at, :])
            k = self.k[t, at, :]
            vt = jnp.transpose(self.v[t, at, :])
            outs = []
            for e, qe in enumerate((q0, q1)):
                s = dot_nt(k, qe)
                s = jnp.where(lax.broadcasted_iota(jnp.int32, s.shape, 0) < L, s, -1e30)
                x = jnp.exp(s - jnp.max(s, axis=0, keepdims=True))
                p = (x * (1.0 / jnp.sum(x, axis=0, keepdims=True))).astype(BF16)
                self.pt[(t * self.images + i) * 2 + e] = p
                outs.append(dot(vt[e * 64 : e * 64 + 64, :], p))
            ot = jnp.concatenate(outs, axis=0).astype(BF16)
            self.hot[i, pl.ds(pl.multiple_of(t * 128, 128), 128), :] = ot
            self.ho[t, at, :] = jnp.transpose(ot)

    def w_proj(self):
        return jnp.concatenate(
            [
                jnp.concatenate(
                    [self.g_at[3, h, pl.ds(b * 384, 384), :] for b in range(6)], axis=1)
                for h in range(2)
            ],
            axis=0,
        )

    def project(self):
        @pl.loop(0, self.images)
        def _(i):
            at = pl.ds(pl.multiple_of(i * LP, 16), LP)
            o = jnp.concatenate([self.ho[t, at, :] for t in range(6)], axis=1)
            self.br1[at, :] = dot(o, self.w_proj()) + self.pb[...]

    def second_norm(self):
        def body(at):
            middle = self.mixed[at, :] + self.ls[0:1, :] * self.br1[at, :]
            sc, _ = normed(middle)
            self.n2[at, :] = (sc * self.n2g[...] + self.n2s[...]).astype(BF16)
            self.br2[at, :] = jnp.zeros((48, D), F32)
            self.gn2[at, :] = jnp.zeros((48, D), F32)

        self.row_loop(body)
        self.n2t[...] = jnp.transpose(self.n2[...])

    def feed(self, j, h):
        wd = jnp.concatenate(
            [self.g_ff[j, h, pl.ds(b * 256, 256), :] for b in range(6)], axis=1)
        wu = jnp.concatenate(
            [self.g_ff[j, h, pl.ds(1536 + b * D, D), :] for b in range(2)], axis=1)
        row = h * 6 + j
        pre = dot(self.n2[...], wu) + self.ub[pl.ds(row, 1), :]
        cdf = 0.5 * (1.0 + lax.erf(pre * INV_ROOT2))
        act = (pre * cdf).astype(BF16)
        slope = cdf + pre * jnp.exp(-0.5 * pre * pre) * INV_ROOT2PI
        gp32 = dot_nt(self.gb[...], wd) * slope
        gp = gp32.astype(BF16)
        self.uba[row] = fold(gp.astype(F32))
        self.br2[...] += dot(act, wd)
        self.gn2[...] += dot_nt(gp, wu)
        gwd = dot(jnp.transpose(act), self.gb[...]).astype(BF16)
        gwu = dot(self.n2t[...], gp).astype(BF16)
        for b in range(6):
            self.g_ff[j, h, pl.ds(b * 256, 256), :] = gwd[:, b * 128 : b * 128 + 128]
        for b in range(2):
            self.g_ff[j, h, pl.ds(1536 + b * D, D), :] = gwu[:, b * 128 : b * 128 + 128]

    def middle_back(self):
        ls0, ls1 = self.ls[0:1, :], self.ls[1:2, :]

        def body(at):
            b1 = self.br1[at, :]
            middle = self.mixed[at, :] + ls0 * b1
            sc, inv = normed(middle)
            b2 = self.br2[at, :] + self.db[...]
            self.outp[at, :] = (middle + ls1 * b2).astype(BF16)
            self.br2[at, :] = jnp.zeros((48, D), F32)
            go = self.gout[at, :].astype(F32)
            self.acc(LS1, go * b2)
            self.acc(DB, self.gb[at, :].astype(F32))
            g = self.gn2[at, :]
            self.acc(N2G, g * sc)
            self.acc(N2S, g)
            gm = go + norm_back(g, self.n2g[...], sc, inv)
            self.acc(LS0, gm * b1)
            gb1 = (ls0 * gm).astype(BF16)
            self.gb[at, :] = gb1
            self.acc(PB, gb1.astype(F32))
            self.gn2[at, :] = gm

        self.row_loop(body)

    def output(self):
        self.narrow(self.outp, self.out)

    def proj_back(self):
        @pl.loop(0, self.images)
        def _(i):
            at = pl.ds(pl.multiple_of(i * LP, 16), LP)
            gh = dot_nt(self.gb[at, :], self.w_proj()).astype(BF16)
            for t in range(6):
                self.ho[t, at, :] = gh[:, t * 128 : t * 128 + 128]

    def proj_grad(self, h):
        total = sum(
            dot(self.hot[i, pl.ds(h * 384, 384), :], self.gb[pl.ds(i * LP, LP), :])
            for i in range(self.images))
        for b in range(6):
            self.g_at[3, h, pl.ds(b * 384, 384), :] = total[
                :, b * 128 : b * 128 + 128].astype(BF16)

    def attend_back(self, t):
        for i in range(self.images):
            at = pl.ds(i * LP, LP)
            q0, q1 = self.two(self.q[t, at, :])
            d0, d1 = self.two(self.ho[t, at, :])
            k = self.k[t, at, :]
            v = self.v[t, at, :]
            kt = jnp.transpose(k)
            dq, dk, dv = [], 0.0, 0.0
            for e, (qe, de) in enumerate(((q0, d0), (q1, d1))):
                pb = self.pt[(t * self.images + i) * 2 + e]
                p = pb.astype(F32)
                gp = dot_nt(v, de)
                gs = (p * (gp - jnp.sum(gp * p, axis=0, keepdims=True))).astype(BF16)
                dv = dv + dot(pb, de)
                dk = dk + dot(gs, qe)
                dq.append(dot(kt[e * 64 : e * 64 + 64, :], gs))
            dq = jnp.transpose(jnp.concatenate(dq, axis=0)) * 0.125
            self.dqkv[at, 0:128] = dq.astype(BF16)
            self.dqkv[at, 128:256] = dk.astype(BF16)
            self.dqkv[at, 256:384] = dv.astype(BF16)
        self.qa[t] = fold(self.dqkv[:, 0:128].astype(F32))
        self.qa[8 + t] = fold(self.dqkv[:, 256:384].astype(F32))

    def qkv_back(self, j, h):
        self.br2[...] += dot_nt(self.dqkv[...], self.w_pair(j, h))
        grad = dot(self.n1t[...], self.dqkv[...])
        for p in range(3):
            self.g_at[j, h, pl.ds(p * D, D), :] = grad[
                :, p * 128 : p * 128 + 128].astype(BF16)

    def first_back(self):
        def body(at):
            sc, inv = normed(self.mixed[at, :])
            g = self.br2[at, :]
            self.acc(N1G, g * sc)
            self.acc(N1S, g)
            gx = self.gn2[at, :] + norm_back(g, self.n1g[...], sc, inv)
            mk = wide(self.maskp[at, :]) > 0.5
            self.acc(MTOK, jnp.where(mk, gx, 0.0))
            self.br2[at, :] = jnp.where(mk, 0.0, gx)

        self.row_loop(body)

    def sums(self, vec):
        vec[...] = jnp.zeros_like(vec)
        for s in range(NSUM):
            vec[s : s + 1, :] = jnp.sum(
                self.vacc[pl.ds(s * 8, 8), :], axis=0, keepdims=True)
        for h, (qv, up) in enumerate(((QVO, UPO), (QVX, UPX))):
            for w in range(2):
                for j in range(3):
                    c = w * 384 + j * 128
                    vec[qv : qv + 1, c : c + 128] = jnp.sum(
                        self.qa[8 * w + h * 3 + j], axis=0, keepdims=True)
            for j in range(6):
                c = j % 3 * 256
                vec[up + j // 3 : up + j // 3 + 1, c : c + 256] = jnp.sum(
                    self.uba[h * 6 + j], axis=0, keepdims=True)


def layer_scratch(rows):
    n = rows // L
    padded = n * LP
    v = pltpu.VMEM
    return dict(
        t32=v(((rows + 11 + 15) // 16 * 16 + 0, D), F32),
        mrow=v((128, (rows + 127) // 128 * 128), F32),
        mcol=v(((rows + 127) // 128 * 128, 128), F32),
        maskp=v((padded, 128), F32),
        mixed=v((padded, D), F32),
        gout=v((padded, D), BF16),
        n1=v((padded, D), BF16),
        n1t=v((D, padded), BF16),
        q=v((6, padded, 128), BF16),
        k=v((6, padded, 128), BF16),
        v=v((6, padded, 128), BF16),
        pt=v((6 * n * 2, LP, LP), BF16),
        ho=v((6, padded, 128), BF16),
        hot=v((n, D, LP), BF16),
        br1=v((padded, D), F32),
        n2=v((padded, D), BF16),
        n2t=v((D, padded), BF16),
        gb=v((padded, D), BF16),
        outp=v((padded, D), BF16),
        br2=v((padded, D), F32),
        gn2=v((padded, D), F32),
        dqkv=v((padded, 384), BF16),
        rows8=v((8, D), F32),
        vacc=v((NSUM * 8, D), F32),
        qb=v((16, 128), F32),
        ub=v((12, 256), F32),
        qa=v((16, 8, 128), F32),
        uba=v((12, 8, 256), F32),
    )


FF_ROWS, AT_ROWS = 3072, 2304
CHUNKS = tuple([("g_ff", j, FF_ROWS) for j in range(6)] + [("g_at", j, AT_ROWS) for j in range(4)])


def plan_of(n, bits):
    rows, steps = n // 2, []
    for b in range(1, bits):
        if rows // 2 % 16 == 0:
            rows //= 2
            steps.append((b, rows, True))
        else:
            steps.append((b, rows, False))
    return steps


def land_offsets(bits):
    at, table = 0, {}
    for k, (_, _, n) in enumerate(CHUNKS):
        table[k, "y"] = at
        at += n // 2
        for b, rows, _ in plan_of(n, bits):
            table[k, b] = at
            at += rows
    return table, at


class Links:
    def __init__(self, r, bits):
        self.__dict__.update(r)
        self.bits = bits
        self.dp = lax.axis_index("dp")
        self.half = lax.axis_index("tensor")
        self.bit = [(self.dp // (1 << b)) % 2 for b in range(bits)]
        self.offsets, _ = land_offsets(bits)

    def peer(self, way):
        if way == "y":
            return (self.dp, 1 - self.half)
        return (self.dp + (1 << way) * (1 - 2 * self.bit[way]), self.half)

    def greet(self):
        barrier = pltpu.get_barrier_semaphore()
        ways = ["y"] + list(range(self.bits))
        for way in ways:
            pl.semaphore_signal(barrier, inc=1, device_id=self.peer(way), device_id_type=MESH)
        pl.semaphore_wait(barrier, len(ways))

    def copy(self, src, dst, send, recv, way):
        return pltpu.make_async_remote_copy(
            src_ref=src, dst_ref=dst, send_sem=send, recv_sem=recv,
            device_id=self.peer(way), device_id_type=MESH)

    def load(self, k):
        name, j, n = CHUNKS[k]
        sem = self.load_sem.at[k]
        if name == "g_ff":
            for b in range(6):
                pltpu.make_async_copy(
                    self.w_dn.at[pl.ds(j * 256, 256), pl.ds(b * 128, 128)],
                    self.g_ff.at[j, 0, pl.ds(b * 256, 256)], sem).start()
            for b in range(2):
                pltpu.make_async_copy(
                    self.w_up.at[:, pl.ds(j * 256 + b * 128, 128)],
                    self.g_ff.at[j, 0, pl.ds(1536 + b * D, D)], sem).start()
        elif j < 3:
            for p in range(3):
                pltpu.make_async_copy(
                    self.w_qkv.at[p, :, pl.ds(j * 128, 128)],
                    self.g_at.at[j, 0, pl.ds(p * D, D)], sem).start()
        else:
            for b in range(6):
                pltpu.make_async_copy(
                    self.w_pr.at[:, pl.ds(b * 128, 128)],
                    self.g_at.at[3, 0, pl.ds(b * 384, 384)], sem).start()

    def loaded(self, k):
        name, j, n = CHUNKS[k]
        ref = getattr(self, name).at[j, 0]
        pltpu.make_async_copy(ref, ref, self.load_sem.at[k]).wait()

    def bias(self, stage):
        a = self.copy(self.qvb, self.qvbx, self.b_send.at[0], self.b_recv.at[0], "y")
        b = self.copy(self.upb, self.upbx, self.b_send.at[1], self.b_recv.at[1], "y")
        if stage == 0:
            a.start()
            b.start()
            return
        a.wait()
        b.wait()
        for h, (qv, up) in enumerate(((self.qvb, self.upb), (self.qvbx, self.upbx))):
            for j in range(3):
                for w in range(2):
                    row = 8 * w + h * 3 + j
                    self.qb[row : row + 1, :] = qv[w : w + 1, j * 128 : j * 128 + 128]
            for j in range(6):
                row = h * 6 + j
                self.ub[row : row + 1, :] = up[pl.ds(j * 256, 256)][None, :]

    def gather_copies(self, k):
        name, j, n = CHUNKS[k]
        ref = getattr(self, name)
        piece = n // 16
        core, b1, b2 = self.bit[0], self.bit[1], self.bit[2]
        base = core * (n // 2)

        def make(i, half, off, rows, way):
            def build():
                at = pl.ds(pl.multiple_of(off, 16), rows)
                return self.copy(
                    ref.at[j, half, at], ref.at[j, 1, at],
                    self.w_send.at[k, i], self.w_recv.at[k, i], way)

            return build

        p0 = base + (b2 * 2 + b1) * piece
        p1 = base + n // 4 + (b1 * 2 + b2) * piece
        return [
            make(0, 0, p0, piece, "y"),
            make(1, 0, p1, piece, "y"),
            make(2, 1, p0, piece, 1),
            make(3, 1, p1, piece, 2),
            make(4, 1, base + b2 * 2 * piece, 2 * piece, 2),
            make(5, 1, base + n // 4 + b1 * 2 * piece, 2 * piece, 1),
            make(6, 1, base, n // 2, 0),
        ]

    def gather(self, k, stage):
        c = self.gather_copies(k)
        if stage == 0:
            self.loaded(k)
            c[0]().start()
            c[1]().start()
        elif stage == 1:
            c[0]().wait_recv()
            c[2]().start()
            c[1]().wait_recv()
            c[3]().start()
        elif stage == 2:
            c[2]().wait_recv()
            c[4]().start()
            c[3]().wait_recv()
            c[5]().start()
        elif stage == 3:
            c[4]().wait_recv()
            c[5]().wait_recv()
            c[6]().start()
        elif stage == 4:
            c[6]().wait_recv()
        else:
            for one in c:
                one().wait_send()

    def add(self, dst, dst_at, src, src_at, rows):
        size = next(s for s in (256, 192, 144, 128, 112, 96, 80, 64, 48, 32, 16) if rows % s == 0)

        @pl.loop(0, rows // size)
        def _(b):
            to = pl.ds(pl.multiple_of(dst_at + b * size, 16), size)
            of = pl.ds(pl.multiple_of(src_at + b * size, 16), size)
            total = dst[to, :].astype(F32) + src[of, :].astype(F32)
            dst[to, :] = total.astype(BF16)

    def reduce_copies(self, k):
        name, j, n = CHUNKS[k]
        ref = getattr(self, name)
        land1 = self.land_ff if name == "g_ff" else self.land_at
        own, mine = ref.at[j, 0], self.bit[0] * (n // 2)
        out = []

        def add(src, dst, way, adds):
            i = len(out)

            def build():
                return self.copy(src(), dst(), self.r_send.at[k, i], self.r_recv.at[k, i], way)

            out.append((build, adds))

        def rows_of(r, at, rows):
            return lambda: r.at[pl.ds(pl.multiple_of(at, 16), rows)]

        theirs = (1 - self.bit[0]) * (n // 2)
        add(lambda: ref.at[j, :, pl.ds(pl.multiple_of(theirs, 16), n // 2), :],
            lambda: land1.at[j], 0,
            [(ref.at[j, h], mine, land1.at[j, h], 0, n // 2) for h in range(2)])
        o = self.offsets[k, "y"]
        add(rows_of(ref.at[j, 1], mine, n // 2), rows_of(self.land, o, n // 2), "y",
            [(own, mine, self.land, o, n // 2)])
        back = [(0, mine, n // 2)]
        for b, rows, halves in plan_of(n, self.bits):
            o = self.offsets[k, b]
            if halves:
                away = mine + (1 - self.bit[b]) * rows
                mine = mine + self.bit[b] * rows
                back.append((b, mine, rows))
            else:
                away = mine
            add(rows_of(own, away, rows), rows_of(self.land, o, rows), b,
                [(own, mine, self.land, o, rows)])
        for b, at, rows in back[::-1]:
            add(rows_of(own, at, rows), rows_of(own, at, rows), b, [])
        return out

    def result_copy(self, k):
        name, j, n = CHUNKS[k]
        out = self.o_ff if name == "g_ff" else self.o_at
        return pltpu.make_async_copy(
            getattr(self, name).at[j, 0], out.at[j], self.out_sem.at[k])

    def reduce(self, k, stage):
        steps = self.reduce_copies(k)
        if stage > 0:
            build, adds = steps[stage - 1]
            copy = build()
            copy.wait_recv()
            if adds:
                copy.wait_send()
                way = self.way(stage - 1)
                if way != "y" and self.halving(k, stage - 1):
                    pl.semaphore_signal(
                        self.credit.at[k, way], inc=1, device_id=self.peer(way),
                        device_id_type=MESH)
            for dst, dst_at, src, src_at, rows in adds:
                self.add(dst, dst_at, src, src_at, rows)
        if stage < len(steps):
            if not steps[stage][1]:
                pl.semaphore_wait(self.credit.at[k, self.back_way(k, stage)], 1)
            steps[stage][0]().start()
        else:
            self.result_copy(k).start()

    def way(self, step):
        return (0, "y")[step] if step < 2 else step - 1

    def back_way(self, k, step):
        ways = [0] + [b for b, _, halves in plan_of(CHUNKS[k][2], self.bits) if halves]
        return ways[::-1][step - self.bits - 1]

    def halving(self, k, step):
        plan = plan_of(CHUNKS[k][2], self.bits)
        return step < 2 or step - 2 >= len(plan) or plan[step - 2][2]

    def finish(self, k):
        for i, (build, adds) in enumerate(self.reduce_copies(k)):
            if not adds:
                build().wait_send()
        self.result_copy(k).wait()

    def vec_copy(self, s):
        way = self.way(s)
        return self.copy(self.vb.at[s], self.vr.at[s], self.v_send.at[s], self.v_recv.at[s], way)

    def vec(self, stage):
        if stage > 0:
            s = stage - 1
            self.vec_copy(s).wait_recv()
            if s == 1:
                self.vb[2, 0:NSUM, :] = self.vb[1, 0:NSUM, :] + self.vr[1, 0:NSUM, :]
                self.vb[2, QVO:QVX, :] = self.vb[1, QVO:QVX, :] + self.vr[1, QVX : QVX + 3, :]
                self.vb[2, QVX:NVEC, :] = jnp.zeros((NVEC - QVX, D), F32)
            else:
                self.vb[stage] = self.vb[s] + self.vr[s]
        if stage < self.bits + 1:
            self.vec_copy(stage).start()

    def vec_end(self):
        for s in range(self.bits + 1):
            self.vec_copy(s).wait_send()
        self.o_vec[...] = self.vb[self.bits + 1]


def link_scratch(bits):
    v, dma = pltpu.VMEM, pltpu.SemaphoreType.DMA
    steps = 2 * bits + 1
    return dict(
        g_ff=v((6, 2, FF_ROWS, 128), BF16),
        g_at=v((4, 2, AT_ROWS, 128), BF16),
        land_ff=v((6, 2, FF_ROWS // 2, 128), BF16),
        land_at=v((4, 2, AT_ROWS // 2, 128), BF16),
        land=v((land_offsets(bits)[1], 128), BF16),
        qvbx=v((2, 384), F32),
        upbx=v((1536,), F32),
        vb=v((bits + 2, NVEC, D), F32),
        vr=v((bits + 1, NVEC, D), F32),
        load_sem=dma((10,)),
        out_sem=dma((10,)),
        b_send=dma((2,)),
        b_recv=dma((2,)),
        w_send=dma((10, 7)),
        w_recv=dma((10, 7)),
        r_send=dma((10, steps)),
        r_recv=dma((10, steps)),
        credit=pltpu.SemaphoreType.REGULAR((10, bits)),
        v_send=dma((bits + 1,)),
        v_recv=dma((bits + 1,)),
    )


GATHER_ORDER = (6, 7, 8, 9, 0, 1, 2, 3, 4, 5)


def timeline(bits):
    pieces = [("start", 2.2, None)]
    pieces += [(("qa", t, s), (0.6, 1.5)[s], 6 + t - 3 if s == 0 and t >= 3 else None)
               for t in range(3) for s in range(2)]
    pieces += [("start2", 1.5, None)]
    pieces += [(("qa", t, s), (0.6, 1.5)[s], 6 + t - 3 if s == 0 else None)
               for t in range(3, 6) for s in range(2)]
    pieces += [("project", 1.2, 9), ("second_norm", 4.0, None)]
    pieces += [(("feed", u, 0), 1.95, u // 2 if u % 2 == 0 else None) for u in range(12)]
    pieces += [("middle_back", 4.0, None), ("proj_back", 1.0, None),
               ("proj_grad", 1.6, None)]
    pieces += [(("back", u, s), (1.65, 1.4)[s], None) for u in range(6) for s in range(2)]
    pieces += [("first_back", 2.5, None), ("sums", 1.0, None), ("output", 1.5, None), ("tokens", 1.5, None)]
    after = {("feed", 2 * j + 1, 0): j for j in range(6)}
    after["proj_grad"] = 9
    after.update({("back", 2 * j + 1, 1): 6 + j for j in range(3)})

    rate = 91e3 / 2
    free = {}

    def send(now, way, nbytes):
        if way == 0:
            line, took = "c", nbytes / 480e3
        elif way == "y" or way == 1:
            line, took = way, nbytes / rate
        else:
            line, took = "z", nbytes / rate * (2 if way > 2 else 1)
        begin = max(now, free.get(line, 0.0))
        free[line] = begin + took
        return begin + took + 1.7

    steps = 2 * bits + 1
    order, now = [], 3.0
    w_stage, w_ready = {}, {}
    r_stage, r_ready = {}, {}
    v_stage, v_ready = None, 0.0

    def reduce_bytes(k, stage):
        n = CHUNKS[k][2]
        plan = plan_of(n, bits)
        ways = [(0, n * 256), ("y", n * 128)] + [(b, rows * 256) for b, rows, _ in plan]
        ways += [(b, rows * 256) for b, rows, halves in plan[::-1] if halves] + [(0, n * 128)]
        return ways, ways[stage] if stage < len(ways) else None

    def gather_step(k):
        nonlocal now
        s = w_stage[k]
        n = CHUNKS[k][2]
        piece = n // 16 * 256
        order.append(("w", k, s))
        now = max(now, w_ready[k]) + 0.25
        if s == 0:
            w_ready[k] = send(now, "y", 2 * piece)
        elif s == 1:
            w_ready[k] = max(send(now, 1, piece), send(now, 2, piece))
        elif s == 2:
            w_ready[k] = max(send(now, 2, 2 * piece), send(now, 1, 2 * piece))
        elif s == 3:
            w_ready[k] = send(now, 0, n // 2 * 256)
        else:
            w_ready[k] = now
        w_stage[k] = s + 1

    def reduce_step(k):
        nonlocal now
        s = r_stage[k]
        ways, this = reduce_bytes(k, s)
        order.append(("r", k, s))
        now = max(now, r_ready[k]) + 0.2
        if 1 <= s <= 2 + len(plan_of(CHUNKS[k][2], bits)):
            now += ways[s - 1][1] / 2e6
        if this is None:
            del r_stage[k]
            return
        r_ready[k] = send(now, *this)
        r_stage[k] = s + 1

    def vec_step():
        nonlocal now, v_stage, v_ready
        order.append(("v", v_stage))
        now = max(now, v_ready) + 0.2
        if v_stage == bits + 1:
            v_stage = None
            return
        way = (0, "y")[v_stage] if v_stage < 2 else v_stage - 1
        v_ready = send(now, way, NVEC * D * 4)
        v_stage += 1

    def poll():
        again = True
        while again:
            again = False
            for k in sorted(r_stage, key=lambda k: (min(r_stage[k], 2), r_ready[k])):
                if r_ready[k] + SLACK <= now:
                    reduce_step(k)
                    again = True
                    break
            if again:
                continue
            for k in GATHER_ORDER:
                if k in w_stage and w_stage[k] <= 4 and w_ready[k] + SLACK <= now:
                    gather_step(k)
                    again = True
                    break
            if not again and v_stage is not None and v_ready + SLACK <= now:
                vec_step()
                again = True

    for k in GATHER_ORDER:
        w_stage[k], w_ready[k] = 0, 0.0
        gather_step(k)
    for piece, took, needs in pieces:
        poll()
        if needs is not None:
            while w_stage[needs] <= 4:
                first = min((k for k in w_stage if w_stage[k] <= 4),
                            key=lambda k: (w_ready[k], GATHER_ORDER.index(k)))
                if w_ready[first] > w_ready[needs]:
                    first = needs
                gather_step(first)
            order.append(("w", needs, 5))
        order.append(("c", piece))
        now += took
        if piece in after:
            k = after[piece]
            r_stage[k], r_ready[k] = 0, now
        if piece == "sums":
            v_stage, v_ready = 0, now
    while r_stage or v_stage is not None:
        k = min(r_stage, key=lambda k: r_ready[k]) if r_stage else None
        if v_stage is not None and (k is None or v_ready <= r_ready[k]):
            vec_step()
        else:
            reduce_step(k)
    return order, now


SLACK = 0.3


def layer_kernel(bits, rows, names, *refs):
    r = dict(zip(names, refs))
    y = Layer(r, rows)
    links = Links(r, bits)
    order, _ = timeline(bits)
    for k in GATHER_ORDER:
        links.load(k)
    y.vectors()
    links.greet()
    links.bias(0)

    def link_step(op):
        if op[0] == "w":
            links.gather(op[1], op[2])
        elif op[0] == "r":
            links.reduce(op[1], op[2])
        else:
            links.vec(op[1])

    def attend(t, s):
        if s == 0:
            y.qkv(lax.rem(t, 3), t // 3)
        else:
            y.attend(t)

    def feed(u, s):
        y.feed(u // 2, 1 - lax.rem(u, 2))

    def back(u, s):
        j, h = u // 2, 1 - lax.rem(u, 2)
        if s == 0:
            y.attend_back(h * 3 + j)
        else:
            y.qkv_back(j, h)

    loops = {"qa": (attend, 2), "feed": (feed, 1), "back": (back, 2)}

    def proj_grad():
        y.proj_grad(1)
        y.proj_grad(0)

    single = {
        "start": y.start,
        "start2": y.start2,
        "project": y.project,
        "second_norm": y.second_norm,
        "middle_back": y.middle_back,
        "proj_back": y.proj_back,
        "proj_grad": proj_grad,
        "first_back": y.first_back,
        "sums": lambda: y.sums(links.vb.at[0]),
        "output": y.output,
        "tokens": lambda: y.narrow(y.br2, y.gtok),
    }

    at = 0
    first_pass = True
    while at < len(order):
        op = order[at]
        if op[0] != "c":
            link_step(op)
            at += 1
            continue
        if isinstance(op[1], str):
            if op[1] == "start":
                single["start"]()
                links.bias(1)
            else:
                single[op[1]]()
            at += 1
            continue
        kind = op[1][0]
        body, slots = loops[kind]
        end, last = at, at
        while end < len(order):
            o = order[end]
            if o[0] == "c":
                if isinstance(o[1], str) or o[1][0] != kind:
                    break
                last = end
            end += 1
        before = {}
        pending = []
        for o in order[at : last + 1]:
            if o[0] == "c":
                before[o[1][1], o[1][2]] = pending
                pending = []
            else:
                pending.append(o)
        low = op[1][1]
        high = order[last][1][1] + 1

        @pl.loop(low, high)
        def _(t):
            for s in range(slots):
                for u in range(low, high):
                    if before[u, s]:
                        @pl.when(t == u)
                        def _(ops=before[u, s]):
                            for o in ops:
                                link_step(o)
                body(t, s)

        at = last + 1
    for k in range(10):
        links.finish(k)
    links.vec_end()


INPUTS = ("tok", "mask", "in_mtok", "in_n1g", "in_n1s", "qvb", "in_pb", "ls", "in_n2g", "in_n2s",
          "upb", "in_db", "cot", "w_qkv", "w_pr", "w_up", "w_dn")
OUTPUTS = ("out", "gtok", "o_ff", "o_at", "o_vec")


def finish_kernel(ff, at, vec, o1, o2, p1, p2, wu, wd, wq, wp, mt, g1, s1, qv, pb, ls, g2, s2, ub, db):
    j = pl.program_id(0)
    for b in range(6):
        wd[:, b * 128 : b * 128 + 128] = ff[0, b * 256 : b * 256 + 256, :].astype(F32)
    for b in range(2):
        wu[:, b * 128 : b * 128 + 128] = ff[
            0, 1536 + b * D : 1536 + b * D + D, :].astype(F32)

    @pl.when(j < 3)
    def _():
        for p in range(3):
            wq[p] = at[0, p * D : p * D + D, :].astype(F32)

    @pl.when(j == 3)
    def _():
        for b in range(6):
            wp[:, b * 128 : b * 128 + 128] = at[0, b * 384 : b * 384 + 384, :].astype(F32)

    @pl.when(j == 4)
    def _():
        p1[...] = o1[...]
        p2[...] = o2[...]

    @pl.when(j == 0)
    def _():
        for ref, row in ((mt, MTOK), (g1, N1G), (s1, N1S), (pb, PB), (g2, N2G), (s2, N2S),
                         (db, DB)):
            ref[...] = vec[row, :]
        ls[...] = vec[LS0 : LS1 + 1, :]
        for w in range(2):
            qv[w : w + 1, :] = vec[QVO : QVO + 1, w * 384 : w * 384 + 384]
            ub[pl.ds(w * D, D)] = vec[UPO + w, :]


def local(dp, tokens, patch_mask, mask_token, norm1_gain, norm1_shift, w_qkv, qv_bias, w_proj,
          proj_bias, layer_scales, norm2_gain, norm2_shift, w_up, up_bias, w_down, down_bias,
          cotangent):
    bits = dp.bit_length() - 1
    rows = tokens.shape[0]
    scratch = {**layer_scratch(rows), **link_scratch(bits)}
    vmem, hbm = pl.BlockSpec(memory_space=pltpu.VMEM), pl.BlockSpec(memory_space=pl.ANY)
    shape = jax.ShapeDtypeStruct
    out, gtok, ff, at, vec = pl.pallas_call(
        functools.partial(layer_kernel, bits, rows, INPUTS + OUTPUTS + tuple(scratch)),
        name="layer",
        in_specs=[vmem] * 13 + [hbm] * 4,
        out_specs=[vmem, vmem, hbm, hbm, vmem],
        out_shape=[
            shape((rows, D), BF16),
            shape((rows, D), BF16),
            shape((6, FF_ROWS, 128), BF16),
            shape((4, AT_ROWS, 128), BF16),
            shape((NVEC, D), F32),
        ],
        scratch_shapes=list(scratch.values()),
        compiler_params=pltpu.CompilerParams(
            collective_id=0, has_side_effects=True, vmem_limit_bytes=63 * 2**20),
        cost_estimate=pl.CostEstimate(
            flops=27 * 10**9, bytes_accessed=20 * 10**6, transcendentals=10**7),
    )(
        tokens, patch_mask, mask_token, norm1_gain, norm1_shift, qv_bias, proj_bias,
        layer_scales, norm2_gain, norm2_shift, up_bias, down_bias, cotangent, w_qkv, w_proj,
        w_up, w_down,
    )
    one = shape((D,), F32)
    flat = pl.BlockSpec((D,), lambda j: (0,))
    whole = pl.BlockSpec((rows, D), lambda j: (0, 0))
    out, gtok, wu, wd, wq, wp, mt, g1, s1, qv, pb, ls, g2, s2, ub, db = pl.pallas_call(
        finish_kernel,
        name="finish",
        grid=(6,),
        in_specs=[
            pl.BlockSpec((1, FF_ROWS, 128), lambda j: (j, 0, 0)),
            pl.BlockSpec((1, AT_ROWS, 128), lambda j: (jnp.minimum(j, 3), 0, 0)),
            pl.BlockSpec((NVEC, D), lambda j: (0, 0)),
            whole, whole,
        ],
        out_specs=[
            whole, whole,
            pl.BlockSpec((D, 256), lambda j: (0, j)),
            pl.BlockSpec((256, D), lambda j: (j, 0)),
            pl.BlockSpec((3, D, 128), lambda j: (0, 0, jnp.minimum(j, 2))),
            pl.BlockSpec((384, D), lambda j: (0, 0)),
            flat, flat, flat,
            pl.BlockSpec((2, 384), lambda j: (0, 0)),
            flat,
            pl.BlockSpec((2, D), lambda j: (0, 0)),
            flat, flat,
            pl.BlockSpec((2 * D,), lambda j: (0,)),
            flat,
        ],
        out_shape=[
            shape((rows, D), BF16), shape((rows, D), BF16),
            shape((D, 1536), F32), shape((1536, D), F32), shape((3, D, 384), F32),
            shape((384, D), F32), one, one, one, shape((2, 384), F32), one, shape((2, D), F32),
            one, one, shape((2 * D,), F32), one,
        ],
    )(ff, at, vec, out, gtok)
    return out, gtok, mt, g1, s1, wq, qv, wp, pb, ls, g2, s2, wu, ub, wd, db


def solution(mesh):
    rows2, both = P(("dp", "tensor"), None), P(("dp", "tensor"))
    return jax.shard_map(
        functools.partial(local, mesh.shape["dp"]),
        mesh=mesh,
        in_specs=(
            rows2, both, P(), P(), P(), P(None, None, "tensor"), P(None, "tensor"),
            P("tensor", None), P(), P(), P(), P(), P(None, "tensor"), P("tensor"),
            P("tensor", None), P(), rows2,
        ),
        out_specs=(
            rows2, rows2, P(), P(), P(), P(None, None, "tensor"), P(None, "tensor"),
            P("tensor", None), P(), P(), P(), P(), P(None, "tensor"), P("tensor"),
            P("tensor", None), P(),
        ),
        check_vma=False,
    )
```

time: 629 us -> 175 us (0.28)
  blocking collectives: 200 us -> 0 us
  Pallas kernels: 0 us -> 172 us
  waiting for transfers between devices: 151 us -> 0 us
  local copies, waits for them, and re-layouts: 123 us -> 0 us
  matrix products: 80.9 us -> 0 us
  other arithmetic: 42.2 us -> 0 us
  between operations: 15.3 us -> 0.82 us
  starting transfers between devices: 11.1 us -> 0 us
    pallas_call x0 -> x2, Pallas kernels: none -> 172 us  [the longest x1 162 us: local(): pl.pallas_call(functools.partial(layer_kernel, bits, rows, INPUTS + OUTPU...]
    psum x2 -> x0, blocking collectives: 103 us -> none  [the longest x1 63.8 us: local(): lax.psum((grad_w_qkv, grad_qv_bias, grad_w_proj, grad_w_up, grad_up_bias,...]
    unnamed x3 -> x0, blocking collectives: 97.1 us -> none
    dot_general x18 -> x0, matrix products: 80.9 us -> none  [the longest x1 8.17 us: local(): jnp.einsum('rd,rf->df', normed2_all, grad_pre, preferred_element_type=jnp...]
    all_gather x4 -> x0, waiting for transfers between devices: 77.3 us -> none  [the longest x1 30.1 us: local(): normed1_all = lax.all_gather(normed1, 'tensor', axis=0, tiled=True)]
    psum x1 -> x0, waiting for transfers between devices: 71.9 us -> none  [local(): lax.psum((grad_w_qkv, grad_qv_bias, grad_w_proj, grad_w_up, grad_up_bias,...]
    unnamed x119 -> x0, local copies, waits for them, and re-layouts: 63.3 us -> none
    convert_element_type x10 -> x0, local copies, waits for them, and re-layouts: 35.7 us -> none  [the longest x2 8.48 us: local(): grad_values = jnp.einsum('bhqk,bqhe->bkhe', probs_low, grad_head_split, p...]
  transfers between devices with their start and end apart: 9 -> 0, of which waited for: 6 -> 0; matrix products, arithmetic and copies ran while one was open for 30% -> 0% of each run, Pallas kernels for 0% -> 0%
where the time goes in v1:
time: 175 us; the launch traced here: 173 us
  Pallas kernels  172 us (98%)
    pallas_call x1, Pallas kernels, local(): pl.pallas_call(functools.partial(layer_kernel, bits, rows, INPUTS + OUTPU...  162 us
    pallas_call x1, Pallas kernels, local(): pl.pallas_call(finish_kernel, name='finish', grid=(6,), in_specs=[pl.Bloc...  10.8 us

profile of v1, /device:TPU:0, one launch (start us, length us, event | category | flops | bytes accessed | tf_op | source)
XLA Modules:
  0.0 173.3 jit_solution(11491481681931950142)
XLA Ops:
  0.7 161.6 %layer.1 = (bf16[591,768]{1,0:T(8,128)(2,1)}, bf16[591,768]{1,0:T(8,128)(2,1)}, bf16[6,3072,128]{2,1,0:T(8,128)(2,1)}, bf16[4,2304,128]{2,1,0:T(8,128)(2,1)}, f32[16,768]{1,0:T(8,128)}) custom-call(bf16[591,768]{1,0:T(8,128)(2,1)} %refs_0_.1, s32[591]{0:T(1024)} %refs_1_.1, f32[768]{0:T(1024)} %refs_2_.1, f32[768]{0:T(1024)} %refs_3_.1, f32[768]{0:T(1024)} %refs_4_.1, ...), custom_call_target="tpu_custom_call" | custom-call | flops 27000000512 | bytes 20000000 | tf_op jit(solution)/shard_map/layer/pallas_call | solution.py:972
  162.3 10.8 %finish.1 = (bf16[591,768]{1,0:T(8,128)(2,1)}, bf16[591,768]{1,0:T(8,128)(2,1)}, f32[768,1536]{1,0:T(8,128)}, f32[1536,768]{1,0:T(8,128)}, f32[3,768,384]{2,1,0:...) custom-call(bf16[6,3072,128]{2,1,0:T(8,128)(2,1)} %get-tuple-element, ...), custom_call_target="tpu_custom_call" | custom-call | tf_op jit(solution)/shard_map/finish/pallas_call | solution.py:997

commit v2 on v1

--- a/solution.py
+++ b/solution.py
@@ -96,10 +96,9 @@
         if left:
             dst[n * 16 : self.rows, :] = self.t32[n * 16 : self.rows, :].astype(BF16)
 
-    def row_loop(self, body):
-        @pl.loop(0, self.padded // 48)
-        def _(b):
-            body(pl.ds(pl.multiple_of(b * 48, 48), 48))
+    def bands(self, i):
+        for r, n in BLOCKS:
+            yield pl.ds(pl.multiple_of(i * LP + r, 16), n), n
 
     def acc(self, at, x):
         self.vacc[pl.ds(at * 8, 8), :] += fold(x)
@@ -118,6 +117,7 @@
         self.mcol[...] = jnp.transpose(self.mrow[...])
         self.t32[pl.ds(rows, self.t32.shape[0] - rows), :] = jnp.zeros(
             (self.t32.shape[0] - rows, D), F32)
+        self.io_copy(0).wait()
         self.widen(self.tok)
         for i in range(self.images):
             for r, n in BLOCKS:
@@ -137,6 +137,8 @@
 
     def start2(self):
         self.n1t[...] = jnp.transpose(self.n1[...])
+        self.io_copy(1).wait()
+        self.clear()
         self.widen(self.cot)
         for i in range(self.images):
             for r, n in BLOCKS:
@@ -173,7 +175,9 @@
             outs = []
             for e, qe in enumerate((q0, q1)):
                 s = dot_nt(k, qe)
-                s = jnp.where(lax.broadcasted_iota(jnp.int32, s.shape, 0) < L, s, -1e30)
+                tail = s[LP - 16 :]
+                keep = lax.broadcasted_iota(jnp.int32, tail.shape, 0) < L - (LP - 16)
+                s = jnp.concatenate([s[: LP - 16], jnp.where(keep, tail, -1e30)], axis=0)
                 x = jnp.exp(s - jnp.max(s, axis=0, keepdims=True))
                 p = (x * (1.0 / jnp.sum(x, axis=0, keepdims=True))).astype(BF16)
                 self.pt[(t * self.images + i) * 2 + e] = p
@@ -193,21 +197,21 @@
         )
 
     def project(self):
-        @pl.loop(0, self.images)
-        def _(i):
-            at = pl.ds(pl.multiple_of(i * LP, 16), LP)
-            o = jnp.concatenate([self.ho[t, at, :] for t in range(6)], axis=1)
-            self.br1[at, :] = dot(o, self.w_proj()) + self.pb[...]
+        o = jnp.concatenate([self.ho[t] for t in range(6)], axis=1)
+        self.br1[...] = dot(o, self.w_proj()) + self.pb[...]
 
     def second_norm(self):
-        def body(at):
-            middle = self.mixed[at, :] + self.ls[0:1, :] * self.br1[at, :]
-            sc, _ = normed(middle)
-            self.n2[at, :] = (sc * self.n2g[...] + self.n2s[...]).astype(BF16)
-            self.br2[at, :] = jnp.zeros((48, D), F32)
-            self.gn2[at, :] = jnp.zeros((48, D), F32)
-
-        self.row_loop(body)
+        for i in range(self.images):
+            for at, rows in self.bands(i):
+                middle = self.mixed[at, :] + self.ls[0:1, :] * self.br1[at, :]
+                sc, _ = normed(middle)
+                self.n2[at, :] = (sc * self.n2g[...] + self.n2s[...]).astype(BF16)
+
+    def clear(self):
+        self.br2[...] = jnp.zeros_like(self.br2)
+        self.gn2[...] = jnp.zeros_like(self.gn2)
+
+    def turn(self):
         self.n2t[...] = jnp.transpose(self.n2[...])
 
     def feed(self, j, h):
@@ -232,16 +236,15 @@
         for b in range(2):
             self.g_ff[j, h, pl.ds(1536 + b * D, D), :] = gwu[:, b * 128 : b * 128 + 128]
 
-    def middle_back(self):
+    def middle_back(self, i):
         ls0, ls1 = self.ls[0:1, :], self.ls[1:2, :]
-
-        def body(at):
+        for at, rows in self.bands(i):
             b1 = self.br1[at, :]
             middle = self.mixed[at, :] + ls0 * b1
             sc, inv = normed(middle)
             b2 = self.br2[at, :] + self.db[...]
             self.outp[at, :] = (middle + ls1 * b2).astype(BF16)
-            self.br2[at, :] = jnp.zeros((48, D), F32)
+            self.br2[at, :] = jnp.zeros((rows, D), F32)
             go = self.gout[at, :].astype(F32)
             self.acc(LS1, go * b2)
             self.acc(DB, self.gb[at, :].astype(F32))
@@ -255,18 +258,23 @@
             self.acc(PB, gb1.astype(F32))
             self.gn2[at, :] = gm
 
-        self.row_loop(body)
+    def io_copy(self, i):
+        src, dst = ((self.h_tok, self.tok), (self.h_cot, self.cot), (self.tok, self.h_out),
+                    (self.cot, self.h_gtok))[i]
+        return pltpu.make_async_copy(src, dst, self.io_sem.at[i])
 
     def output(self):
-        self.narrow(self.outp, self.out)
+        self.narrow(self.outp, self.tok)
+        self.io_copy(2).start()
+
+    def tokens(self):
+        self.narrow(self.br2, self.cot)
+        self.io_copy(3).start()
 
     def proj_back(self):
-        @pl.loop(0, self.images)
-        def _(i):
-            at = pl.ds(pl.multiple_of(i * LP, 16), LP)
-            gh = dot_nt(self.gb[at, :], self.w_proj()).astype(BF16)
-            for t in range(6):
-                self.ho[t, at, :] = gh[:, t * 128 : t * 128 + 128]
+        gh = dot_nt(self.gb[...], self.w_proj()).astype(BF16)
+        for t in range(6):
+            self.ho[t] = gh[:, t * 128 : t * 128 + 128]
 
     def proj_grad(self, h):
         total = sum(
@@ -307,8 +315,8 @@
             self.g_at[j, h, pl.ds(p * D, D), :] = grad[
                 :, p * 128 : p * 128 + 128].astype(BF16)
 
-    def first_back(self):
-        def body(at):
+    def first_back(self, i):
+        for at, _ in self.bands(i):
             sc, inv = normed(self.mixed[at, :])
             g = self.br2[at, :]
             self.acc(N1G, g * sc)
@@ -317,8 +325,6 @@
             mk = wide(self.maskp[at, :]) > 0.5
             self.acc(MTOK, jnp.where(mk, gx, 0.0))
             self.br2[at, :] = jnp.where(mk, 0.0, gx)
-
-        self.row_loop(body)
 
     def sums(self, vec):
         vec[...] = jnp.zeros_like(vec)
@@ -342,6 +348,9 @@
     padded = n * LP
     v = pltpu.VMEM
     return dict(
+        tok=v((rows, D), BF16),
+        cot=v((rows, D), BF16),
+        io_sem=pltpu.SemaphoreType.DMA((4,)),
         t32=v(((rows + 11 + 15) // 16 * 16 + 0, D), F32),
         mrow=v((128, (rows + 127) // 128 * 128), F32),
         mcol=v(((rows + 127) // 128 * 128, 128), F32),
@@ -377,26 +386,57 @@
 CHUNKS = tuple([("g_ff", j, FF_ROWS) for j in range(6)] + [("g_at", j, AT_ROWS) for j in range(4)])
 
 
-def plan_of(n, bits):
-    rows, steps = n // 2, []
-    for b in range(1, bits):
-        if rows // 2 % 16 == 0:
+Y_FIRST, Z_FIRST = (0, "y", 1, 2, 3), (0, 2, "y", 1, 3)
+CUTS = {
+    0: ((5, (0, 'y', 1, 13, 12), -31), (6, (0, 1, 2, 'y', 13), -60), (1, (0, 'y', 1, 12, 13), -41),),
+    1: ((3, (0, 2, 1, 3, 'y'), -2), (3, (0, 'y', 1, 2, 13), 4), (6, (0, 'y', 1, 2, 13), 50),),
+    2: ((6, (0, 1, 'y', 2, 13), 40), (6, (0, 'y', 1, 2, 13), 47),),
+    3: ((4, (0, 2, 1, 13, 'y'), -10), (8, (0, 'y', 2, 1, 13), -49),),
+    4: ((10, (0, 'y', 1, 2, 13), 27), (2, (0, 'y', 2, 1, 13), -42),),
+    5: ((1, (0, 1, 2, 13, 'y'), 14), (11, (0, 1, 'y', 2, 13), -38),),
+    9: ((2, (0, 2, 1, 'y', 3), -16), (7, (0, 'y', 1, 2, 13), -24),),
+    6: ((9, (0, 'y', 1, 2, 13), 23),),
+    7: ((9, (0, 'y', 1, 2, 13), 6),),
+    8: ((4, (0, 1, 'y', 2, 13), 5), (5, (0, 'y', 2, 1, 13), 2),),
+}
+
+
+def parts_of():
+    out = []
+    for k, cuts in CUTS.items():
+        at = 0
+        for units, order, weight in cuts:
+            out.append((k, at, units * 256, order, weight))
+            at += units * 256
+    return tuple(out)
+
+
+PARTS = parts_of()
+
+
+def steps_of(part, bits):
+    _, _, rows, order, _ = part
+    order = [w for w in order if w == "y" or w % 10 < bits] + list(range(4, bits))
+    both, out = True, []
+    for way in order:
+        if way == "y":
+            both = False
+            out.append((way, False, rows, False))
+        elif way < 10 and rows // 2 % 16 == 0:
             rows //= 2
-            steps.append((b, rows, True))
+            out.append((way, both, rows, True))
         else:
-            steps.append((b, rows, False))
-    return steps
+            out.append((way % 10, both, rows, False))
+    return out
 
 
 def land_offsets(bits):
-    at, table = 0, {}
-    for k, (_, _, n) in enumerate(CHUNKS):
-        table[k, "y"] = at
-        at += n // 2
-        for b, rows, _ in plan_of(n, bits):
-            table[k, b] = at
-            at += rows
-    return table, at
+    sizes, table = [0, 0], {}
+    for p, part in enumerate(PARTS):
+        for i, (_, both, rows, _) in enumerate(steps_of(part, bits)):
+            table[p, i] = sizes[both]
+            sizes[both] += rows
+    return table, sizes
 
 
 class Links:
@@ -471,59 +511,32 @@
                 row = h * 6 + j
                 self.ub[row : row + 1, :] = up[pl.ds(j * 256, 256)][None, :]
 
-    def gather_copies(self, k):
+    def gather_copy(self, k, i):
         name, j, n = CHUNKS[k]
         ref = getattr(self, name)
-        piece = n // 16
-        core, b1, b2 = self.bit[0], self.bit[1], self.bit[2]
-        base = core * (n // 2)
-
-        def make(i, half, off, rows, way):
-            def build():
-                at = pl.ds(pl.multiple_of(off, 16), rows)
-                return self.copy(
-                    ref.at[j, half, at], ref.at[j, 1, at],
-                    self.w_send.at[k, i], self.w_recv.at[k, i], way)
-
-            return build
-
-        p0 = base + (b2 * 2 + b1) * piece
-        p1 = base + n // 4 + (b1 * 2 + b2) * piece
-        return [
-            make(0, 0, p0, piece, "y"),
-            make(1, 0, p1, piece, "y"),
-            make(2, 1, p0, piece, 1),
-            make(3, 1, p1, piece, 2),
-            make(4, 1, base + b2 * 2 * piece, 2 * piece, 2),
-            make(5, 1, base + n // 4 + b1 * 2 * piece, 2 * piece, 1),
-            make(6, 1, base, n // 2, 0),
-        ]
+        way, rows = gather_plan(k)[i]
+        off = self.bit[0] * (n // 2)
+        size = n // 2
+        for further in ROUTES[k][:0:-1][: len(ROUTES[k]) - max(i, 1)]:
+            size //= 2
+            off = off + self.bit[further] * size
+        at = pl.ds(pl.multiple_of(off, 16), rows)
+        return self.copy(
+            ref.at[j, int(i > 0), at], ref.at[j, 1, at],
+            self.w_send.at[k, i], self.w_recv.at[k, i], way)
 
     def gather(self, k, stage):
-        c = self.gather_copies(k)
+        copies = len(gather_plan(k))
+        if stage < 0:
+            for i in range(copies):
+                self.gather_copy(k, i).wait_send()
+            return
         if stage == 0:
             self.loaded(k)
-            c[0]().start()
-            c[1]().start()
-        elif stage == 1:
-            c[0]().wait_recv()
-            c[2]().start()
-            c[1]().wait_recv()
-            c[3]().start()
-        elif stage == 2:
-            c[2]().wait_recv()
-            c[4]().start()
-            c[3]().wait_recv()
-            c[5]().start()
-        elif stage == 3:
-            c[4]().wait_recv()
-            c[5]().wait_recv()
-            c[6]().start()
-        elif stage == 4:
-            c[6]().wait_recv()
         else:
-            for one in c:
-                one().wait_send()
+            self.gather_copy(k, stage - 1).wait_recv()
+        if stage < copies:
+            self.gather_copy(k, stage).start()
 
     def add(self, dst, dst_at, src, src_at, rows):
         size = next(s for s in (256, 192, 144, 128, 112, 96, 80, 64, 48, 32, 16) if rows % s == 0)
@@ -535,93 +548,79 @@
             total = dst[to, :].astype(F32) + src[of, :].astype(F32)
             dst[to, :] = total.astype(BF16)
 
-    def reduce_copies(self, k):
-        name, j, n = CHUNKS[k]
+    def reduce_steps(self, p):
+        part = PARTS[p]
+        k, first, rows = part[:3]
+        name, j, _ = CHUNKS[k]
         ref = getattr(self, name)
-        land1 = self.land_ff if name == "g_ff" else self.land_at
-        own, mine = ref.at[j, 0], self.bit[0] * (n // 2)
-        out = []
-
-        def add(src, dst, way, adds):
+        own = ref.at[j, 0]
+        at, out, back = first, [], []
+
+        def add(way, src, dst, adds, halves):
             i = len(out)
 
             def build():
-                return self.copy(src(), dst(), self.r_send.at[k, i], self.r_recv.at[k, i], way)
-
-            out.append((build, adds))
+                return self.copy(src(), dst(), self.r_send.at[p, i], self.r_recv.at[p, i], way)
+
+            out.append((way, build, adds, halves))
 
         def rows_of(r, at, rows):
             return lambda: r.at[pl.ds(pl.multiple_of(at, 16), rows)]
 
-        theirs = (1 - self.bit[0]) * (n // 2)
-        add(lambda: ref.at[j, :, pl.ds(pl.multiple_of(theirs, 16), n // 2), :],
-            lambda: land1.at[j], 0,
-            [(ref.at[j, h], mine, land1.at[j, h], 0, n // 2) for h in range(2)])
-        o = self.offsets[k, "y"]
-        add(rows_of(ref.at[j, 1], mine, n // 2), rows_of(self.land, o, n // 2), "y",
-            [(own, mine, self.land, o, n // 2)])
-        back = [(0, mine, n // 2)]
-        for b, rows, halves in plan_of(n, self.bits):
-            o = self.offsets[k, b]
+        def both_of(r, at, rows):
+            return lambda: r.at[:, pl.ds(pl.multiple_of(at, 16), rows)]
+
+        for way, both, rows, halves in steps_of(part, self.bits):
+            o = self.offsets[p, len(out)]
+            away = at
             if halves:
-                away = mine + (1 - self.bit[b]) * rows
-                mine = mine + self.bit[b] * rows
-                back.append((b, mine, rows))
+                away = at + (1 - self.bit[way]) * rows
+                at = at + self.bit[way] * rows
+                back.append((way, at, rows))
+            if both:
+                add(way, both_of(ref.at[j], away, rows), both_of(self.land2, o, rows),
+                    [(ref.at[j, h], at, self.land2.at[h], o, rows) for h in range(2)], halves)
             else:
-                away = mine
-            add(rows_of(own, away, rows), rows_of(self.land, o, rows), b,
-                [(own, mine, self.land, o, rows)])
-        for b, at, rows in back[::-1]:
-            add(rows_of(own, at, rows), rows_of(own, at, rows), b, [])
+                src = ref.at[j, 1] if way == "y" else own
+                add(way, rows_of(src, away, rows), rows_of(self.land, o, rows),
+                    [(own, at, self.land, o, rows)], halves)
+        for way, at, rows in back[::-1]:
+            add(way, rows_of(own, at, rows), rows_of(own, at, rows), [], False)
         return out
 
-    def result_copy(self, k):
-        name, j, n = CHUNKS[k]
+    def result_copy(self, p):
+        k, first, rows = PARTS[p][:3]
+        name, j, _ = CHUNKS[k]
         out = self.o_ff if name == "g_ff" else self.o_at
+        at = pl.ds(first, rows)
         return pltpu.make_async_copy(
-            getattr(self, name).at[j, 0], out.at[j], self.out_sem.at[k])
-
-    def reduce(self, k, stage):
-        steps = self.reduce_copies(k)
+            getattr(self, name).at[j, 0, at], out.at[j, at], self.out_sem.at[p])
+
+    def reduce(self, p, stage):
+        steps = self.reduce_steps(p)
         if stage > 0:
-            build, adds = steps[stage - 1]
+            way, build, adds, halves = steps[stage - 1]
             copy = build()
             copy.wait_recv()
-            if adds:
-                copy.wait_send()
-                way = self.way(stage - 1)
-                if way != "y" and self.halving(k, stage - 1):
-                    pl.semaphore_signal(
-                        self.credit.at[k, way], inc=1, device_id=self.peer(way),
-                        device_id_type=MESH)
-            for dst, dst_at, src, src_at, rows in adds:
-                self.add(dst, dst_at, src, src_at, rows)
+            copy.wait_send()
+            if halves:
+                pl.semaphore_signal(
+                    self.credit.at[p, way], inc=1, device_id=self.peer(way), device_id_type=MESH)
+            for one in adds:
+                self.add(*one)
         if stage < len(steps):
-            if not steps[stage][1]:
-                pl.semaphore_wait(self.credit.at[k, self.back_way(k, stage)], 1)
-            steps[stage][0]().start()
+            way, build, adds, _ = steps[stage]
+            if not adds:
+                pl.semaphore_wait(self.credit.at[p, way], 1)
+            build().start()
         else:
-            self.result_copy(k).start()
-
-    def way(self, step):
-        return (0, "y")[step] if step < 2 else step - 1
-
-    def back_way(self, k, step):
-        ways = [0] + [b for b, _, halves in plan_of(CHUNKS[k][2], self.bits) if halves]
-        return ways[::-1][step - self.bits - 1]
-
-    def halving(self, k, step):
-        plan = plan_of(CHUNKS[k][2], self.bits)
-        return step < 2 or step - 2 >= len(plan) or plan[step - 2][2]
-
-    def finish(self, k):
-        for i, (build, adds) in enumerate(self.reduce_copies(k)):
-            if not adds:
-                build().wait_send()
-        self.result_copy(k).wait()
+            self.result_copy(p).start()
+
+    def finish(self, p):
+        self.result_copy(p).wait()
 
     def vec_copy(self, s):
-        way = self.way(s)
+        way = (0, "y")[s] if s < 2 else s - 1
         return self.copy(self.vb.at[s], self.vr.at[s], self.v_send.at[s], self.v_recv.at[s], way)
 
     def vec(self, stage):
@@ -646,171 +645,167 @@
 def link_scratch(bits):
     v, dma = pltpu.VMEM, pltpu.SemaphoreType.DMA
     steps = 2 * bits + 1
+    parts = len(PARTS)
+    land = land_offsets(bits)[1]
     return dict(
         g_ff=v((6, 2, FF_ROWS, 128), BF16),
         g_at=v((4, 2, AT_ROWS, 128), BF16),
-        land_ff=v((6, 2, FF_ROWS // 2, 128), BF16),
-        land_at=v((4, 2, AT_ROWS // 2, 128), BF16),
-        land=v((land_offsets(bits)[1], 128), BF16),
+        land2=v((2, land[1], 128), BF16),
+        land=v((land[0], 128), BF16),
         qvbx=v((2, 384), F32),
         upbx=v((1536,), F32),
         vb=v((bits + 2, NVEC, D), F32),
         vr=v((bits + 1, NVEC, D), F32),
         load_sem=dma((10,)),
-        out_sem=dma((10,)),
+        out_sem=dma((parts,)),
         b_send=dma((2,)),
         b_recv=dma((2,)),
-        w_send=dma((10, 7)),
-        w_recv=dma((10, 7)),
-        r_send=dma((10, steps)),
-        r_recv=dma((10, steps)),
-        credit=pltpu.SemaphoreType.REGULAR((10, bits)),
+        w_send=dma((10, 4)),
+        w_recv=dma((10, 4)),
+        r_send=dma((parts, steps)),
+        r_recv=dma((parts, steps)),
+        credit=pltpu.SemaphoreType.REGULAR((parts, bits)),
         v_send=dma((bits + 1,)),
         v_recv=dma((bits + 1,)),
     )
 
 
-GATHER_ORDER = (6, 7, 8, 9, 0, 1, 2, 3, 4, 5)
-
-
-def timeline(bits):
-    pieces = [("start", 2.2, None)]
-    pieces += [(("qa", t, s), (0.6, 1.5)[s], 6 + t - 3 if s == 0 and t >= 3 else None)
-               for t in range(3) for s in range(2)]
-    pieces += [("start2", 1.5, None)]
-    pieces += [(("qa", t, s), (0.6, 1.5)[s], 6 + t - 3 if s == 0 else None)
-               for t in range(3, 6) for s in range(2)]
-    pieces += [("project", 1.2, 9), ("second_norm", 4.0, None)]
-    pieces += [(("feed", u, 0), 1.95, u // 2 if u % 2 == 0 else None) for u in range(12)]
-    pieces += [("middle_back", 4.0, None), ("proj_back", 1.0, None),
-               ("proj_grad", 1.6, None)]
-    pieces += [(("back", u, s), (1.65, 1.4)[s], None) for u in range(6) for s in range(2)]
-    pieces += [("first_back", 2.5, None), ("sums", 1.0, None), ("output", 1.5, None), ("tokens", 1.5, None)]
+ROUTES = (('y', 1), ('y', 2), ('y', 2, 1), ('y', 1), ('y', 1, 2), ('y', 1, 2), ('y', 1, 2), ('y', 2, 1), ('y', 2), ('y', 2, 1))
+GATHER_ORDER = (6, 7, 9, 8, 2, 0, 1, 4, 5, 3)
+
+
+def gather_plan(k):
+    rows, ways = CHUNKS[k][2] // 2, ROUTES[k]
+    n = len(ways)
+    steps = [("y", rows >> (n - 1))]
+    steps += [(way, rows >> (n - 1 - i)) for i, way in enumerate(ways[1:])]
+    return steps + [(0, rows)]
+
+
+SLACK, STEP, BACKLOG = 0.2, 0.05, 2.455
+HOPS = {0: 0.9, "y": 2.2, 1: 2.2, 2: 2.2}
+FAR_HOP = 2.7
+LINK, CORES, SUMS, MESSAGE, LOADS, ENTRY = 45.5e3, 480e3, 2.4e6, 0.1, 3.0e6, 3.8
+LINES = {0: (("c", 1),), "y": (("y", 1),), 1: (("x", 1),), 2: (("z", 1),)}
+FAR_LINES = (("z", 1), ("mid", 2))
+
+
+def compute_pieces():
+    out = [("start", 0.5, None)]
+    out += [(("qa", t, s), (0.57, 1.45)[s], None) for t in range(3) for s in range(2)]
+    out += [("start2", 1.7, None)]
+    out += [(("qa", t, s), (0.57, 1.45)[s], 3 + t if s == 0 else None)
+            for t in range(3, 6) for s in range(2)]
+    out += [("project", 1.6, 9), ("second_norm", 0.8, None), ("turn", 0.6, None)]
+    out += [(("feed", u, 0), 1.96, u // 2 if u % 2 == 0 else None) for u in range(12)]
+    out += [(("middle_back", i, 0), 1.2, None) for i in range(3)]
+    out += [("proj_back", 1.0, None), ("proj_grad", 1.6, None)]
+    out += [(("back", u, s), (1.62, 1.4)[s], None) for u in range(6) for s in range(2)]
+    out += [(("first_back", i, 0), 0.8, None) for i in range(3)]
+    out += [("sums", 0.6, None), ("output", 0.6, None), ("tokens", 0.6, None)]
     after = {("feed", 2 * j + 1, 0): j for j in range(6)}
     after["proj_grad"] = 9
     after.update({("back", 2 * j + 1, 1): 6 + j for j in range(3)})
-
-    rate = 91e3 / 2
-    free = {}
-
-    def send(now, way, nbytes):
-        if way == 0:
-            line, took = "c", nbytes / 480e3
-        elif way == "y" or way == 1:
-            line, took = way, nbytes / rate
-        else:
-            line, took = "z", nbytes / rate * (2 if way > 2 else 1)
-        begin = max(now, free.get(line, 0.0))
-        free[line] = begin + took
-        return begin + took + 1.7
-
-    steps = 2 * bits + 1
-    order, now = [], 3.0
-    w_stage, w_ready = {}, {}
-    r_stage, r_ready = {}, {}
-    v_stage, v_ready = None, 0.0
-
-    def reduce_bytes(k, stage):
-        n = CHUNKS[k][2]
-        plan = plan_of(n, bits)
-        ways = [(0, n * 256), ("y", n * 128)] + [(b, rows * 256) for b, rows, _ in plan]
-        ways += [(b, rows * 256) for b, rows, halves in plan[::-1] if halves] + [(0, n * 128)]
-        return ways, ways[stage] if stage < len(ways) else None
-
-    def gather_step(k):
-        nonlocal now
-        s = w_stage[k]
-        n = CHUNKS[k][2]
-        piece = n // 16 * 256
-        order.append(("w", k, s))
-        now = max(now, w_ready[k]) + 0.25
-        if s == 0:
-            w_ready[k] = send(now, "y", 2 * piece)
-        elif s == 1:
-            w_ready[k] = max(send(now, 1, piece), send(now, 2, piece))
-        elif s == 2:
-            w_ready[k] = max(send(now, 2, 2 * piece), send(now, 1, 2 * piece))
-        elif s == 3:
-            w_ready[k] = send(now, 0, n // 2 * 256)
-        else:
-            w_ready[k] = now
-        w_stage[k] = s + 1
-
-    def reduce_step(k):
-        nonlocal now
-        s = r_stage[k]
-        ways, this = reduce_bytes(k, s)
-        order.append(("r", k, s))
-        now = max(now, r_ready[k]) + 0.2
-        if 1 <= s <= 2 + len(plan_of(CHUNKS[k][2], bits)):
-            now += ways[s - 1][1] / 2e6
-        if this is None:
-            del r_stage[k]
+    return out, after
+
+
+class Timeline:
+    def __init__(self, bits, log=None):
+        self.log = log or (lambda *a: None)
+        self.now, self.order, self.tasks = ENTRY, [], {}
+        self.free = {line: 0.0 for line in ("c", "y", "x", "z", "mid")}
+        self.moves, self.adds = {}, {}
+        for k in range(10):
+            self.moves["w", k] = [(way, rows * 256) for way, rows in gather_plan(k)]
+        for p, part in enumerate(PARTS):
+            there = steps_of(part, bits)
+            self.adds["r", p] = [rows * 256 * (1 + both) for _, both, rows, _ in there]
+            self.moves["r", p] = [
+                (way, n) for (way, *_), n in zip(there, self.adds["r", p])
+            ] + [(way, rows * 256) for way, _, rows, halves in there[::-1] if halves]
+        self.moves["v", 0] = [
+            (way, NVEC * D * 4) for way in (0, "y") + tuple(range(1, bits))]
+        self.left = {
+            key: [sum(self.took(*m) + HOPS.get(m[0], FAR_HOP) for m in moves[i:])
+                  for i in range(len(moves) + 1)]
+            for key, moves in self.moves.items()}
+
+    def took(self, way, nbytes):
+        return nbytes / CORES if way == 0 else nbytes / LINK + MESSAGE
+
+    def urgency(self, key):
+        if key[0] == "w":
+            return 1000 - GATHER_ORDER.index(key[1]) * 10 + self.tasks[key][0]
+        weight = PARTS[key[1]][4] if key[0] == "r" else 0
+        return self.left[key][self.tasks[key][0]] + weight
+
+    def opens(self, key):
+        stage, ready = self.tasks[key]
+        if stage < len(self.moves[key]):
+            way = self.moves[key][stage][0]
+            if way != 0:
+                for line, _ in LINES.get(way, FAR_LINES):
+                    ready = max(ready, self.free[line] - BACKLOG)
+        return ready
+
+    def step(self, key):
+        stage, ready = self.tasks[key]
+        self.order.append(key + (stage,))
+        self.log("op", self.now, key, stage, ready)
+        self.now = max(self.now, ready) + STEP
+        if 0 < stage <= len(self.adds.get(key, ())):
+            self.now += self.adds[key][stage - 1] / SUMS
+        if stage == len(self.moves[key]):
+            del self.tasks[key]
             return
-        r_ready[k] = send(now, *this)
-        r_stage[k] = s + 1
-
-    def vec_step():
-        nonlocal now, v_stage, v_ready
-        order.append(("v", v_stage))
-        now = max(now, v_ready) + 0.2
-        if v_stage == bits + 1:
-            v_stage = None
-            return
-        way = (0, "y")[v_stage] if v_stage < 2 else v_stage - 1
-        v_ready = send(now, way, NVEC * D * 4)
-        v_stage += 1
-
-    def poll():
-        again = True
-        while again:
-            again = False
-            for k in sorted(r_stage, key=lambda k: (min(r_stage[k], 2), r_ready[k])):
-                if r_ready[k] + SLACK <= now:
-                    reduce_step(k)
-                    again = True
-                    break
-            if again:
-                continue
-            for k in GATHER_ORDER:
-                if k in w_stage and w_stage[k] <= 4 and w_ready[k] + SLACK <= now:
-                    gather_step(k)
-                    again = True
-                    break
-            if not again and v_stage is not None and v_ready + SLACK <= now:
-                vec_step()
-                again = True
-
-    for k in GATHER_ORDER:
-        w_stage[k], w_ready[k] = 0, 0.0
-        gather_step(k)
-    for piece, took, needs in pieces:
-        poll()
-        if needs is not None:
-            while w_stage[needs] <= 4:
-                first = min((k for k in w_stage if w_stage[k] <= 4),
-                            key=lambda k: (w_ready[k], GATHER_ORDER.index(k)))
-                if w_ready[first] > w_ready[needs]:
-                    first = needs
-                gather_step(first)
-            order.append(("w", needs, 5))
-        order.append(("c", piece))
-        now += took
-        if piece in after:
-            k = after[piece]
-            r_stage[k], r_ready[k] = 0, now
-        if piece == "sums":
-            v_stage, v_ready = 0, now
-    while r_stage or v_stage is not None:
-        k = min(r_stage, key=lambda k: r_ready[k]) if r_stage else None
-        if v_stage is not None and (k is None or v_ready <= r_ready[k]):
-            vec_step()
-        else:
-            reduce_step(k)
-    return order, now
-
-
-SLACK = 0.3
+        way, nbytes = self.moves[key][stage]
+        lines = LINES.get(way, FAR_LINES)
+        begin = max([self.now] + [self.free[line] for line, _ in lines])
+        for line, load in lines:
+            self.free[line] = begin + self.took(way, nbytes) * load
+            self.log("x", line, begin, self.free[line])
+        done = max(self.free[line] for line, _ in lines)
+        self.tasks[key] = (stage + 1, done + HOPS.get(way, FAR_HOP))
+
+    def poll(self, slack):
+        while True:
+            ready = [key for key in self.tasks if self.opens(key) + slack <= self.now]
+            if not ready:
+                return
+            self.step(max(ready, key=self.urgency))
+
+    def wait(self):
+        self.now = max(self.now, min(self.opens(key) for key in self.tasks) + 1e-6)
+        self.poll(0.0)
+
+    def run(self):
+        loaded = ENTRY
+        for k in GATHER_ORDER:
+            loaded += CHUNKS[k][2] * 256 / LOADS
+            self.tasks["w", k] = (0, loaded)
+        pieces, after = compute_pieces()
+        for piece, took, needs in pieces:
+            self.poll(SLACK)
+            if needs is not None:
+                while ("w", needs) in self.tasks:
+                    self.wait()
+                self.order.append(("w", needs, -1))
+            self.order.append(("c", piece))
+            self.log("c", self.now, piece)
+            self.now += took
+            if piece in after:
+                for p, part in enumerate(PARTS):
+                    if part[0] == after[piece]:
+                        self.tasks["r", p] = (0, self.now)
+            if piece == "sums":
+                self.tasks["v", 0] = (0, self.now)
+        while self.tasks:
+            self.wait()
+        return self.order, self.now
+
+
+def timeline(bits, log=None):
+    return Timeline(bits, log).run()
 
 
 def layer_kernel(bits, rows, names, *refs):
@@ -818,8 +813,10 @@
     y = Layer(r, rows)
     links = Links(r, bits)
     order, _ = timeline(bits)
+    y.io_copy(0).start()
     for k in GATHER_ORDER:
         links.load(k)
+    y.io_copy(1).start()
     y.vectors()
     links.greet()
     links.bias(0)
@@ -830,7 +827,7 @@
         elif op[0] == "r":
             links.reduce(op[1], op[2])
         else:
-            links.vec(op[1])
+            links.vec(op[2])
 
     def attend(t, s):
         if s == 0:
@@ -848,7 +845,13 @@
         else:
             y.qkv_back(j, h)
 
-    loops = {"qa": (attend, 2), "feed": (feed, 1), "back": (back, 2)}
+    loops = {
+        "qa": (attend, 2),
+        "feed": (feed, 1),
+        "middle_back": (lambda i, s: y.middle_back(i), 1),
+        "back": (back, 2),
+        "first_back": (lambda i, s: y.first_back(i), 1),
+    }
 
     def proj_grad():
         y.proj_grad(1)
@@ -859,13 +862,12 @@
         "start2": y.start2,
         "project": y.project,
         "second_norm": y.second_norm,
-        "middle_back": y.middle_back,
+        "turn": y.turn,
         "proj_back": y.proj_back,
         "proj_grad": proj_grad,
-        "first_back": y.first_back,
         "sums": lambda: y.sums(links.vb.at[0]),
         "output": y.output,
-        "tokens": lambda: y.narrow(y.br2, y.gtok),
+        "tokens": y.tokens,
     }
 
     at = 0
@@ -917,14 +919,16 @@
                 body(t, s)
 
         at = last + 1
-    for k in range(10):
-        links.finish(k)
+    for i in (2, 3):
+        y.io_copy(i).wait()
+    for p in range(len(PARTS)):
+        links.finish(p)
     links.vec_end()
 
 
-INPUTS = ("tok", "mask", "in_mtok", "in_n1g", "in_n1s", "qvb", "in_pb", "ls", "in_n2g", "in_n2s",
-          "upb", "in_db", "cot", "w_qkv", "w_pr", "w_up", "w_dn")
-OUTPUTS = ("out", "gtok", "o_ff", "o_at", "o_vec")
+INPUTS = ("h_tok", "mask", "in_mtok", "in_n1g", "in_n1s", "qvb", "in_pb", "ls", "in_n2g", "in_n2s",
+          "upb", "in_db", "h_cot", "w_qkv", "w_pr", "w_up", "w_dn")
+OUTPUTS = ("h_out", "h_gtok", "o_ff", "o_at", "o_vec")
 
 
 def finish_kernel(ff, at, vec, o1, o2, p1, p2, wu, wd, wq, wp, mt, g1, s1, qv, pb, ls, g2, s2, ub, db):
@@ -972,8 +976,8 @@
     out, gtok, ff, at, vec = pl.pallas_call(
         functools.partial(layer_kernel, bits, rows, INPUTS + OUTPUTS + tuple(scratch)),
         name="layer",
-        in_specs=[vmem] * 13 + [hbm] * 4,
-        out_specs=[vmem, vmem, hbm, hbm, vmem],
+        in_specs=[hbm] + [vmem] * 11 + [hbm] * 5,
+        out_specs=[hbm, hbm, hbm, hbm, vmem],
         out_shape=[
             shape((rows, D), BF16),
             shape((rows, D), BF16),

time: 175 us -> 149 us (0.85)
  Pallas kernels: 172 us -> 148 us
    pallas_call x1, Pallas kernels: 162 us -> 137 us  [local(): pl.pallas_call(functools.partial(layer_kernel, bits, rows, INPUTS + OUTPU...]
where the time goes in v2:
time: 149 us
  Pallas kernels  148 us (99%)
    pallas_call x1, Pallas kernels, local(): pl.pallas_call(functools.partial(layer_kernel, bits, rows, INPUTS + OUTPU...  137 us
    pallas_call x1, Pallas kernels, local(): pl.pallas_call(finish_kernel, name='finish', grid=(6,), in_specs=[pl.Bloc...  10.8 us

profile of v2, /device:TPU:0, one launch (start us, length us, event | category | flops | bytes accessed | tf_op | source)
XLA Modules:
  0.0 148.8 jit_solution(18162567171752074628)
XLA Ops:
  0.7 137.1 %layer.1 = (bf16[591,768]{1,0:T(8,128)(2,1)}, bf16[591,768]{1,0:T(8,128)(2,1)}, bf16[6,3072,128]{2,1,0:T(8,128)(2,1)}, bf16[4,2304,128]{2,1,0:T(8,128)(2,1)}, f32[16,768]{1,0:T(8,128)}) custom-call(bf16[591,768]{1,0:T(8,128)(2,1)} %refs_0_.1, s32[591]{0:T(1024)} %refs_1_.1, f32[768]{0:T(1024)} %refs_2_.1, f32[768]{0:T(1024)} %refs_3_.1, f32[768]{0:T(1024)} %refs_4_.1, ...), custom_call_target="tpu_custom_call" | custom-call | flops 27000000512 | bytes 20000000 | tf_op jit(solution)/shard_map/layer/pallas_call | solution.py:976
  137.8 10.8 %finish.1 = (bf16[591,768]{1,0:T(8,128)(2,1)}, bf16[591,768]{1,0:T(8,128)(2,1)}, f32[768,1536]{1,0:T(8,128)}, f32[1536,768]{1,0:T(8,128)}, f32[3,768,384]{2,1,0:...) custom-call(bf16[6,3072,128]{2,1,0:T(8,128)(2,1)} %get-tuple-element, ...), custom_call_target="tpu_custom_call" | custom-call | tf_op jit(solution)/shard_map/finish/pallas_call | solution.py:1001

commit v3 on v2

--- a/solution.py
+++ b/solution.py
@@ -59,6 +59,7 @@
 
 
 VECTORS = ("mtok", "n1g", "n1s", "pb", "n2g", "n2s", "db")
+SMALL = VECTORS + ("mask", "qvb", "ls", "upb")
 
 
 class Layer:
@@ -103,8 +104,15 @@
     def acc(self, at, x):
         self.vacc[pl.ds(at * 8, 8), :] += fold(x)
 
+    def small_copy(self, i):
+        name = SMALL[i]
+        return pltpu.make_async_copy(
+            getattr(self, "h_" + name), getattr(self, "in_" + name), self.small_sem.at[i])
+
     def vectors(self):
-        for name in ("mtok", "n1g", "n1s", "pb", "n2g", "n2s", "db"):
+        for i in range(len(SMALL)):
+            self.small_copy(i).wait()
+        for name in VECTORS:
             self.__dict__[name] = self.rows8.at[pl.ds(VECTORS.index(name), 1), :]
             self.rows8[VECTORS.index(name), :] = self.__dict__["in_" + name][...]
 
@@ -112,7 +120,7 @@
         self.vacc[...] = jnp.zeros_like(self.vacc)
         rows = self.rows
         self.mrow[...] = jnp.zeros_like(self.mrow)
-        flags = jnp.where(self.mask[...] == 1, 1.0, 0.0).astype(F32)[None, :]
+        flags = jnp.where(self.in_mask[...] == 1, 1.0, 0.0).astype(F32)[None, :]
         self.mrow[:, pl.ds(0, rows)] = jnp.broadcast_to(flags, (128, rows))
         self.mcol[...] = jnp.transpose(self.mrow[...])
         self.t32[pl.ds(rows, self.t32.shape[0] - rows), :] = jnp.zeros(
@@ -146,7 +154,7 @@
                 to = pl.ds(LP * i + r, n)
                 go = self.t32[at, :] * wide(self.maskp[to, :])
                 self.gout[to, :] = go.astype(BF16)
-                self.gb[to, :] = (self.ls[1:2, :] * go).astype(BF16)
+                self.gb[to, :] = (self.in_ls[1:2, :] * go).astype(BF16)
 
     def w_pair(self, j, h):
         return jnp.concatenate(
@@ -203,7 +211,7 @@
     def second_norm(self):
         for i in range(self.images):
             for at, rows in self.bands(i):
-                middle = self.mixed[at, :] + self.ls[0:1, :] * self.br1[at, :]
+                middle = self.mixed[at, :] + self.in_ls[0:1, :] * self.br1[at, :]
                 sc, _ = normed(middle)
                 self.n2[at, :] = (sc * self.n2g[...] + self.n2s[...]).astype(BF16)
 
@@ -237,13 +245,13 @@
             self.g_ff[j, h, pl.ds(1536 + b * D, D), :] = gwu[:, b * 128 : b * 128 + 128]
 
     def middle_back(self, i):
-        ls0, ls1 = self.ls[0:1, :], self.ls[1:2, :]
+        ls0, ls1 = self.in_ls[0:1, :], self.in_ls[1:2, :]
         for at, rows in self.bands(i):
             b1 = self.br1[at, :]
             middle = self.mixed[at, :] + ls0 * b1
             sc, inv = normed(middle)
             b2 = self.br2[at, :] + self.db[...]
-            self.outp[at, :] = (middle + ls1 * b2).astype(BF16)
+            self.n2[at, :] = (middle + ls1 * b2).astype(BF16)
             self.br2[at, :] = jnp.zeros((rows, D), F32)
             go = self.gout[at, :].astype(F32)
             self.acc(LS1, go * b2)
@@ -264,7 +272,7 @@
         return pltpu.make_async_copy(src, dst, self.io_sem.at[i])
 
     def output(self):
-        self.narrow(self.outp, self.tok)
+        self.narrow(self.n2, self.tok)
         self.io_copy(2).start()
 
     def tokens(self):
@@ -351,6 +359,12 @@
         tok=v((rows, D), BF16),
         cot=v((rows, D), BF16),
         io_sem=pltpu.SemaphoreType.DMA((4,)),
+        small_sem=pltpu.SemaphoreType.DMA((len(SMALL),)),
+        **{"in_" + name: v((D,), F32) for name in VECTORS},
+        in_mask=v((rows,), jnp.int32),
+        in_qvb=v((2, 384), F32),
+        in_ls=v((2, D), F32),
+        in_upb=v((1536,), F32),
         t32=v(((rows + 11 + 15) // 16 * 16 + 0, D), F32),
         mrow=v((128, (rows + 127) // 128 * 128), F32),
         mcol=v(((rows + 127) // 128 * 128, 128), F32),
@@ -369,7 +383,6 @@
         n2=v((padded, D), BF16),
         n2t=v((D, padded), BF16),
         gb=v((padded, D), BF16),
-        outp=v((padded, D), BF16),
         br2=v((padded, D), F32),
         gn2=v((padded, D), F32),
         dqkv=v((padded, 384), BF16),
@@ -388,16 +401,16 @@
 
 Y_FIRST, Z_FIRST = (0, "y", 1, 2, 3), (0, 2, "y", 1, 3)
 CUTS = {
-    0: ((5, (0, 'y', 1, 13, 12), -31), (6, (0, 1, 2, 'y', 13), -60), (1, (0, 'y', 1, 12, 13), -41),),
-    1: ((3, (0, 2, 1, 3, 'y'), -2), (3, (0, 'y', 1, 2, 13), 4), (6, (0, 'y', 1, 2, 13), 50),),
-    2: ((6, (0, 1, 'y', 2, 13), 40), (6, (0, 'y', 1, 2, 13), 47),),
-    3: ((4, (0, 2, 1, 13, 'y'), -10), (8, (0, 'y', 2, 1, 13), -49),),
-    4: ((10, (0, 'y', 1, 2, 13), 27), (2, (0, 'y', 2, 1, 13), -42),),
-    5: ((1, (0, 1, 2, 13, 'y'), 14), (11, (0, 1, 'y', 2, 13), -38),),
-    9: ((2, (0, 2, 1, 'y', 3), -16), (7, (0, 'y', 1, 2, 13), -24),),
-    6: ((9, (0, 'y', 1, 2, 13), 23),),
-    7: ((9, (0, 'y', 1, 2, 13), 6),),
-    8: ((4, (0, 1, 'y', 2, 13), 5), (5, (0, 'y', 2, 1, 13), 2),),
+    0: ((3, (0, 'y', 'F', 'M', 11), -44), (6, (0, 1, 'y', 'F', 'MM'), -11), (3, (0, 'y', 11, 'F', 'MM'), -8),),
+    1: ((1, (0, 'y', 'F', 11, 'MM'), -54), (3, (0, 'y', 'F', 'M', 11), -8), (8, (0, 1, 'y', 'F', 'MM'), -31),),
+    2: ((4, (0, 1, 'y', 'F', 'MM'), -23), (8, (0, 'y', 1, 'F', 'MM'), -27),),
+    3: ((3, (0, 'y', 11, 'F', 'MM'), 45), (4, (0, 1, 'y', 'F', 'MM'), -3), (3, (0, 'F', 'M', 'y', 11), -6), (2, (0, 'F', 'M', 'y', 11), -60),),
+    4: ((9, (0, 1, 'F', 'M', 'y'), -20), (3, (0, 'y', 1, 'F', 'MM'), -39),),
+    5: ((7, (0, 'y', 1, 'F', 'MM'), -10), (5, (0, 'y', 1, 'F', 'MM'), 28),),
+    9: ((9, (0, 'y', 1, 'F', 'MM'), -26),),
+    6: ((4, (0, 'y', 1, 'F', 'M'), -43), (5, (0, 'y', 2, 1, 13), -14),),
+    7: ((4, (0, 'y', 1, 'F', 'MM'), 35), (5, (0, 2, 'y', 1, 13), 32),),
+    8: ((2, (0, 'F', 'M', 'y', 11), 7), (5, (0, 'y', 1, 'F', 'MM'), 1), (2, (0, 'y', 1, 'F', 'MM'), -18),),
 }
 
 
@@ -416,24 +429,29 @@
 
 def steps_of(part, bits):
     _, _, rows, order, _ = part
-    order = [w for w in order if w == "y" or w % 10 < bits] + list(range(4, bits))
-    both, out = True, []
+    order = list(order) + list(range(4, bits))
+    both, role, out = True, "all", []
     for way in order:
         if way == "y":
             both = False
-            out.append((way, False, rows, False))
-        elif way < 10 and rows // 2 % 16 == 0:
+            out.append((way, False, rows, "all", role))
+        elif way == "F":
+            out.append((way, both, rows, "fold", "fold"))
+            role = "inner"
+        elif way == "MM" or (way != "M" and way >= 10):
+            out.append(("M" if way == "MM" else way - 10, both, rows, "all", role))
+        elif rows // 2 % 16 == 0:
             rows //= 2
-            out.append((way, both, rows, True))
+            out.append((way, both, rows, "half", role))
         else:
-            out.append((way % 10, both, rows, False))
+            out.append((way, both, rows, "all", role))
     return out
 
 
 def land_offsets(bits):
     sizes, table = [0, 0], {}
     for p, part in enumerate(PARTS):
-        for i, (_, both, rows, _) in enumerate(steps_of(part, bits)):
+        for i, (_, both, rows, *_) in enumerate(steps_of(part, bits)):
             table[p, i] = sizes[both]
             sizes[both] += rows
     return table, sizes
@@ -446,16 +464,22 @@
         self.dp = lax.axis_index("dp")
         self.half = lax.axis_index("tensor")
         self.bit = [(self.dp // (1 << b)) % 2 for b in range(bits)]
+        self.inner = self.bit[2] != self.bit[3]
+        self.outer = self.bit[2] == self.bit[3]
         self.offsets, _ = land_offsets(bits)
 
     def peer(self, way):
         if way == "y":
             return (self.dp, 1 - self.half)
+        if way in ("M", "MM"):
+            return (self.dp + 4 * (1 - 2 * self.bit[2]) + 8 * (1 - 2 * self.bit[3]), self.half)
+        if way in ("F", "U"):
+            way = 2
         return (self.dp + (1 << way) * (1 - 2 * self.bit[way]), self.half)
 
     def greet(self):
         barrier = pltpu.get_barrier_semaphore()
-        ways = ["y"] + list(range(self.bits))
+        ways = ["y", "M"] + list(range(self.bits))
         for way in ways:
             pl.semaphore_signal(barrier, inc=1, device_id=self.peer(way), device_id_type=MESH)
         pl.semaphore_wait(barrier, len(ways))
@@ -494,15 +518,15 @@
         pltpu.make_async_copy(ref, ref, self.load_sem.at[k]).wait()
 
     def bias(self, stage):
-        a = self.copy(self.qvb, self.qvbx, self.b_send.at[0], self.b_recv.at[0], "y")
-        b = self.copy(self.upb, self.upbx, self.b_send.at[1], self.b_recv.at[1], "y")
+        a = self.copy(self.in_qvb, self.qvbx, self.b_send.at[0], self.b_recv.at[0], "y")
+        b = self.copy(self.in_upb, self.upbx, self.b_send.at[1], self.b_recv.at[1], "y")
         if stage == 0:
             a.start()
             b.start()
             return
         a.wait()
         b.wait()
-        for h, (qv, up) in enumerate(((self.qvb, self.upb), (self.qvbx, self.upbx))):
+        for h, (qv, up) in enumerate(((self.in_qvb, self.in_upb), (self.qvbx, self.upbx))):
             for j in range(3):
                 for w in range(2):
                     row = 8 * w + h * 3 + j
@@ -511,32 +535,31 @@
                 row = h * 6 + j
                 self.ub[row : row + 1, :] = up[pl.ds(j * 256, 256)][None, :]
 
-    def gather_copy(self, k, i):
+    def gather_copy(self, k, sub, i):
         name, j, n = CHUNKS[k]
         ref = getattr(self, name)
-        way, rows = gather_plan(k)[i]
-        off = self.bit[0] * (n // 2)
-        size = n // 2
-        for further in ROUTES[k][:0:-1][: len(ROUTES[k]) - max(i, 1)]:
+        ways = ROUTES[k][sub]
+        way, rows = gather_plan(k, sub)[i]
+        size = n // 4
+        off = self.bit[0] * (n // 2) + sub * size
+        for further in ways[:0:-1][: len(ways) - max(i, 1)]:
             size //= 2
             off = off + self.bit[further] * size
         at = pl.ds(pl.multiple_of(off, 16), rows)
         return self.copy(
             ref.at[j, int(i > 0), at], ref.at[j, 1, at],
-            self.w_send.at[k, i], self.w_recv.at[k, i], way)
-
-    def gather(self, k, stage):
-        copies = len(gather_plan(k))
+            self.w_send.at[k * 2 + sub, i], self.w_recv.at[k * 2 + sub, i], way)
+
+    def gather(self, k, sub, stage):
+        copies = len(gather_plan(k, sub))
         if stage < 0:
             for i in range(copies):
-                self.gather_copy(k, i).wait_send()
+                self.gather_copy(k, sub, i).wait_send()
             return
-        if stage == 0:
-            self.loaded(k)
-        else:
-            self.gather_copy(k, stage - 1).wait_recv()
+        if stage > 0:
+            self.gather_copy(k, sub, stage - 1).wait_recv()
         if stage < copies:
-            self.gather_copy(k, stage).start()
+            self.gather_copy(k, sub, stage).start()
 
     def add(self, dst, dst_at, src, src_at, rows):
         size = next(s for s in (256, 192, 144, 128, 112, 96, 80, 64, 48, 32, 16) if rows % s == 0)
@@ -547,6 +570,11 @@
             of = pl.ds(pl.multiple_of(src_at + b * size, 16), size)
             total = dst[to, :].astype(F32) + src[of, :].astype(F32)
             dst[to, :] = total.astype(BF16)
+
+    def when(self, role):
+        if role == "all":
+            return lambda body: body()
+        return pl.when(self.outer if role == "fold" else self.inner)
 
     def reduce_steps(self, p):
         part = PARTS[p]
@@ -555,14 +583,15 @@
         ref = getattr(self, name)
         own = ref.at[j, 0]
         at, out, back = first, [], []
-
-        def add(way, src, dst, adds, halves):
+        other = {"all": "all", "inner": "inner", "fold": "unfold", "unfold": "fold"}
+
+        def add(way, src, dst, adds, kind, role):
             i = len(out)
 
             def build():
-                return self.copy(src(), dst(), self.r_send.at[p, i], self.r_recv.at[p, i], way)
-
-            out.append((way, build, adds, halves))
+                return self.copy(src(), dst(), self.r_send.at[p], self.r_recv.at[p, i], way)
+
+            out.append((way, build, adds, kind, role, other[role]))
 
         def rows_of(r, at, rows):
             return lambda: r.at[pl.ds(pl.multiple_of(at, 16), rows)]
@@ -570,23 +599,29 @@
         def both_of(r, at, rows):
             return lambda: r.at[:, pl.ds(pl.multiple_of(at, 16), rows)]
 
-        for way, both, rows, halves in steps_of(part, self.bits):
+        for way, both, rows, kind, role in steps_of(part, self.bits):
             o = self.offsets[p, len(out)]
             away = at
-            if halves:
-                away = at + (1 - self.bit[way]) * rows
-                at = at + self.bit[way] * rows
-                back.append((way, at, rows))
+            if kind == "half":
+                b = self.bit[3 if way == "M" else way]
+                away = at + (1 - b) * rows
+                at = at + b * rows
+                back.append((way, at, rows, role))
+            elif kind == "fold":
+                back.append(("U", at, rows, "unfold"))
             if both:
                 add(way, both_of(ref.at[j], away, rows), both_of(self.land2, o, rows),
-                    [(ref.at[j, h], at, self.land2.at[h], o, rows) for h in range(2)], halves)
+                    [(ref.at[j, h], at, self.land2.at[h], o, rows) for h in range(2)], kind, role)
             else:
                 src = ref.at[j, 1] if way == "y" else own
                 add(way, rows_of(src, away, rows), rows_of(self.land, o, rows),
-                    [(own, at, self.land, o, rows)], halves)
-        for way, at, rows in back[::-1]:
-            add(way, rows_of(own, at, rows), rows_of(own, at, rows), [], False)
+                    [(own, at, self.land, o, rows)], kind, role)
+        for way, at, rows, role in back[::-1]:
+            add(way, rows_of(own, at, rows), rows_of(own, at, rows), [], "back", role)
         return out
+
+    def credit_of(self, p, way):
+        return self.credit.at[p, {"F": 2, "U": 2, "M": 3}.get(way, way)]
 
     def result_copy(self, p):
         k, first, rows = PARTS[p][:3]
@@ -599,20 +634,35 @@
     def reduce(self, p, stage):
         steps = self.reduce_steps(p)
         if stage > 0:
-            way, build, adds, halves = steps[stage - 1]
-            copy = build()
-            copy.wait_recv()
-            copy.wait_send()
-            if halves:
-                pl.semaphore_signal(
-                    self.credit.at[p, way], inc=1, device_id=self.peer(way), device_id_type=MESH)
-            for one in adds:
-                self.add(*one)
+            way, build, adds, kind, sender, receiver = steps[stage - 1]
+
+            def taken():
+                build().wait_recv()
+
+            def sent():
+                build().wait_send()
+                if kind in ("half", "fold"):
+                    pl.semaphore_signal(
+                        self.credit_of(p, way), inc=1, device_id=self.peer(way),
+                        device_id_type=MESH)
+
+            def summed():
+                for one in adds:
+                    self.add(*one)
+
+            self.when(receiver)(taken)
+            self.when(sender)(sent)
+            if adds:
+                self.when(receiver)(summed)
         if stage < len(steps):
-            way, build, adds, _ = steps[stage]
-            if not adds:
-                pl.semaphore_wait(self.credit.at[p, way], 1)
-            build().start()
+            way, build, adds, kind, sender, receiver = steps[stage]
+
+            def go():
+                if kind == "back":
+                    pl.semaphore_wait(self.credit_of(p, way), 1)
+                build().start()
+
+            self.when(sender)(go)
         else:
             self.result_copy(p).start()
 
@@ -639,7 +689,10 @@
     def vec_end(self):
         for s in range(self.bits + 1):
             self.vec_copy(s).wait_send()
-        self.o_vec[...] = self.vb[self.bits + 1]
+        self.vec_out().start()
+
+    def vec_out(self):
+        return pltpu.make_async_copy(self.vb.at[self.bits + 1], self.o_vec, self.vec_sem.at[0])
 
 
 def link_scratch(bits):
@@ -660,34 +713,37 @@
         out_sem=dma((parts,)),
         b_send=dma((2,)),
         b_recv=dma((2,)),
-        w_send=dma((10, 4)),
-        w_recv=dma((10, 4)),
-        r_send=dma((parts, steps)),
+        w_send=dma((20, 4)),
+        w_recv=dma((20, 4)),
+        r_send=dma((parts,)),
         r_recv=dma((parts, steps)),
         credit=pltpu.SemaphoreType.REGULAR((parts, bits)),
         v_send=dma((bits + 1,)),
+        vec_sem=dma((1,)),
         v_recv=dma((bits + 1,)),
     )
 
 
-ROUTES = (('y', 1), ('y', 2), ('y', 2, 1), ('y', 1), ('y', 1, 2), ('y', 1, 2), ('y', 1, 2), ('y', 2, 1), ('y', 2), ('y', 2, 1))
-GATHER_ORDER = (6, 7, 9, 8, 2, 0, 1, 4, 5, 3)
-
-
-def gather_plan(k):
-    rows, ways = CHUNKS[k][2] // 2, ROUTES[k]
+ROUTES = ((('y', 1, 2), ('y', 2)), (('y', 1, 2), ('y', 2)), (('y', 1, 2), ('y', 1)), (('y', 2, 1), ('y', 1, 2)), (('y', 1, 2), ('y', 2)), (('y',), ('y', 2)), (('y', 2, 1), ('y', 1, 2)), (('y', 2), ('y', 2, 1)), (('y', 1, 2), ('y', 1)), (('y', 2), ('y', 2, 1)))
+GATHER_ORDER = (6, 7, 8, 9, 0, 1, 2, 3, 4, 5)
+
+
+def gather_plan(k, sub):
+    rows, ways = CHUNKS[k][2] // 4, ROUTES[k][sub]
     n = len(ways)
     steps = [("y", rows >> (n - 1))]
     steps += [(way, rows >> (n - 1 - i)) for i, way in enumerate(ways[1:])]
     return steps + [(0, rows)]
 
 
-SLACK, STEP, BACKLOG = 0.2, 0.05, 2.455
-HOPS = {0: 0.9, "y": 2.2, 1: 2.2, 2: 2.2}
+SLACK, STEP, BACKLOG = 0.2, 0.05, 2.372
+HOPS = {0: 0.9, "y": 2.2, 1: 2.2, 2: 2.2, "F": 2.2, "U": 2.2, "M": 2.2}
 FAR_HOP = 2.7
 LINK, CORES, SUMS, MESSAGE, LOADS, ENTRY = 45.5e3, 480e3, 2.4e6, 0.1, 3.0e6, 3.8
-LINES = {0: (("c", 1),), "y": (("y", 1),), 1: (("x", 1),), 2: (("z", 1),)}
-FAR_LINES = (("z", 1), ("mid", 2))
+LINES = {
+    0: (("c", 1),), "y": (("y", 1),), 1: (("x", 1),), 2: (("zi", 1), ("zo", 1)), "F": (("zi", 1),),
+    "U": (("zo", 1),), "M": (("mid", 1),), "MM": (("mid", 1),)}
+FAR_LINES = (("zi", 1), ("zo", 1), ("mid", 2))
 
 
 def compute_pieces():
@@ -713,16 +769,19 @@
     def __init__(self, bits, log=None):
         self.log = log or (lambda *a: None)
         self.now, self.order, self.tasks = ENTRY, [], {}
-        self.free = {line: 0.0 for line in ("c", "y", "x", "z", "mid")}
+        self.free = {line: 0.0 for line in ("c", "y", "x", "zi", "zo", "mid")}
         self.moves, self.adds = {}, {}
         for k in range(10):
-            self.moves["w", k] = [(way, rows * 256) for way, rows in gather_plan(k)]
+            self.moves["l", k] = []
+            for sub in range(2):
+                self.moves["w", k, sub] = [(way, rows * 256) for way, rows in gather_plan(k, sub)]
         for p, part in enumerate(PARTS):
             there = steps_of(part, bits)
-            self.adds["r", p] = [rows * 256 * (1 + both) for _, both, rows, _ in there]
+            self.adds["r", p] = [rows * 256 * (1 + both) for _, both, rows, *_ in there]
             self.moves["r", p] = [
                 (way, n) for (way, *_), n in zip(there, self.adds["r", p])
-            ] + [(way, rows * 256) for way, _, rows, halves in there[::-1] if halves]
+            ] + [("U" if kind == "fold" else way, rows * 256)
+                 for way, _, rows, kind, _ in there[::-1] if kind in ("half", "fold")]
         self.moves["v", 0] = [
             (way, NVEC * D * 4) for way in (0, "y") + tuple(range(1, bits))]
         self.left = {
@@ -734,6 +793,8 @@
         return nbytes / CORES if way == 0 else nbytes / LINK + MESSAGE
 
     def urgency(self, key):
+        if key[0] == "l":
+            return 2000
         if key[0] == "w":
             return 1000 - GATHER_ORDER.index(key[1]) * 10 + self.tasks[key][0]
         weight = PARTS[key[1]][4] if key[0] == "r" else 0
@@ -757,6 +818,9 @@
             self.now += self.adds[key][stage - 1] / SUMS
         if stage == len(self.moves[key]):
             del self.tasks[key]
+            if key[0] == "l":
+                for sub in range(2):
+                    self.tasks["w", key[1], sub] = (0, self.now)
             return
         way, nbytes = self.moves[key][stage]
         lines = LINES.get(way, FAR_LINES)
@@ -782,14 +846,15 @@
         loaded = ENTRY
         for k in GATHER_ORDER:
             loaded += CHUNKS[k][2] * 256 / LOADS
-            self.tasks["w", k] = (0, loaded)
+            self.tasks["l", k] = (0, loaded)
         pieces, after = compute_pieces()
         for piece, took, needs in pieces:
             self.poll(SLACK)
             if needs is not None:
-                while ("w", needs) in self.tasks:
+                mine = (("l", needs), ("w", needs, 0), ("w", needs, 1))
+                while any(key in self.tasks for key in mine):
                     self.wait()
-                self.order.append(("w", needs, -1))
+                self.order += [("w", needs, 0, -1), ("w", needs, 1, -1)]
             self.order.append(("c", piece))
             self.log("c", self.now, piece)
             self.now += took
@@ -813,17 +878,22 @@
     y = Layer(r, rows)
     links = Links(r, bits)
     order, _ = timeline(bits)
+    links.load(GATHER_ORDER[0])
     y.io_copy(0).start()
-    for k in GATHER_ORDER:
+    for i in range(len(SMALL)):
+        y.small_copy(i).start()
+    for k in GATHER_ORDER[1:]:
         links.load(k)
     y.io_copy(1).start()
+    links.greet()
     y.vectors()
-    links.greet()
     links.bias(0)
 
     def link_step(op):
-        if op[0] == "w":
-            links.gather(op[1], op[2])
+        if op[0] == "l":
+            links.loaded(op[1])
+        elif op[0] == "w":
+            links.gather(*op[1:])
         elif op[0] == "r":
             links.reduce(op[1], op[2])
         else:
@@ -919,50 +989,76 @@
                 body(t, s)
 
         at = last + 1
+    links.vec_end()
     for i in (2, 3):
         y.io_copy(i).wait()
     for p in range(len(PARTS)):
         links.finish(p)
-    links.vec_end()
-
-
-INPUTS = ("h_tok", "mask", "in_mtok", "in_n1g", "in_n1s", "qvb", "in_pb", "ls", "in_n2g", "in_n2s",
-          "upb", "in_db", "h_cot", "w_qkv", "w_pr", "w_up", "w_dn")
+    links.vec_out().wait()
+
+
+INPUTS = ("h_tok", "h_mask", "h_mtok", "h_n1g", "h_n1s", "h_qvb", "h_pb", "h_ls", "h_n2g", "h_n2s",
+          "h_upb", "h_db", "h_cot", "w_qkv", "w_pr", "w_up", "w_dn")
 OUTPUTS = ("h_out", "h_gtok", "o_ff", "o_at", "o_vec")
 
 
-def finish_kernel(ff, at, vec, o1, o2, p1, p2, wu, wd, wq, wp, mt, g1, s1, qv, pb, ls, g2, s2, ub, db):
-    j = pl.program_id(0)
-    for b in range(6):
-        wd[:, b * 128 : b * 128 + 128] = ff[0, b * 256 : b * 256 + 256, :].astype(F32)
-    for b in range(2):
-        wu[:, b * 128 : b * 128 + 128] = ff[
-            0, 1536 + b * D : 1536 + b * D + D, :].astype(F32)
-
-    @pl.when(j < 3)
-    def _():
-        for p in range(3):
-            wq[p] = at[0, p * D : p * D + D, :].astype(F32)
-
-    @pl.when(j == 3)
-    def _():
-        for b in range(6):
-            wp[:, b * 128 : b * 128 + 128] = at[0, b * 384 : b * 384 + 384, :].astype(F32)
-
-    @pl.when(j == 4)
-    def _():
-        p1[...] = o1[...]
-        p2[...] = o2[...]
-
-    @pl.when(j == 0)
-    def _():
-        for ref, row in ((mt, MTOK), (g1, N1G), (s1, N1S), (pb, PB), (g2, N2G), (s2, N2S),
-                         (db, DB)):
-            ref[...] = vec[row, :]
-        ls[...] = vec[LS0 : LS1 + 1, :]
-        for w in range(2):
-            qv[w : w + 1, :] = vec[QVO : QVO + 1, w * 384 : w * 384 + 384]
-            ub[pl.ds(w * D, D)] = vec[UPO + w, :]
+FF_OUT, AT_OUT = 6, 4
+
+
+def finish_kernel(ff, at, vec, o1, o2, p1, p2, wu, wd, wq, wp, mt, g1, s1, qv, pb, ls, g2, s2, ub, db,
+                  ff_in, at_in, vec_in, rows_in, up, down, three, proj, mt_v, g1_v, s1_v, qv_v, pb_v,
+                  ls_v, g2_v, s2_v, ub_v, db_v, in_sem, out_sem):
+    order = [("at", j) for j in range(AT_OUT)] + [("ff", j) for j in range(FF_OUT)]
+    loads = [
+        pltpu.make_async_copy(*((ff.at[j], ff_in.at[j]) if kind == "ff" else (at.at[j], at_in.at[j])),
+                              in_sem.at[i])
+        for i, (kind, j) in enumerate(order)]
+    loads += [pltpu.make_async_copy(o, rows_in.at[i], in_sem.at[10 + i])
+              for i, o in enumerate((o1, o2))]
+    sums = pltpu.make_async_copy(vec, vec_in, in_sem.at[12])
+    stores = []
+    for load in loads[:4] + [sums] + loads[4:]:
+        load.start()
+
+    def send(src, dst):
+        copy = pltpu.make_async_copy(src, dst, out_sem.at[len(stores)])
+        copy.start()
+        stores.append(copy)
+
+    for i, ((kind, j), load) in enumerate(zip(order, loads)):
+        load.wait()
+        if kind == "ff":
+            for b in range(6):
+                down[j, :, b * 128 : b * 128 + 128] = ff_in[j, pl.ds(b * 256, 256), :].astype(F32)
+            send(down.at[j], wd.at[pl.ds(j * 256, 256), :])
+            for b in range(2):
+                up[j, :, b * 128 : b * 128 + 128] = ff_in[j, pl.ds(1536 + b * D, D), :].astype(F32)
+            send(up.at[j], wu.at[:, pl.ds(j * 256, 256)])
+        elif j < 3:
+            for p in range(3):
+                three[j, p] = at_in[j, pl.ds(p * D, D), :].astype(F32)
+            send(three.at[j], wq.at[:, :, pl.ds(j * 128, 128)])
+        else:
+            for b in range(6):
+                proj[:, b * 128 : b * 128 + 128] = at_in[j, pl.ds(b * 384, 384), :].astype(F32)
+            send(proj, wp)
+        if i == 4:
+            sums.wait()
+            for ref, row in ((mt_v, MTOK), (g1_v, N1G), (s1_v, N1S), (pb_v, PB), (g2_v, N2G),
+                             (s2_v, N2S), (db_v, DB)):
+                ref[...] = vec_in[row, :]
+            ls_v[...] = vec_in[LS0 : LS1 + 1, :]
+            for w in range(2):
+                qv_v[w : w + 1, :] = vec_in[QVO : QVO + 1, w * 384 : w * 384 + 384]
+                ub_v[pl.ds(w * D, D)] = vec_in[UPO + w, :]
+            for pair in ((mt_v, mt), (g1_v, g1), (s1_v, s1), (qv_v, qv), (pb_v, pb), (ls_v, ls),
+                         (g2_v, g2), (s2_v, s2), (ub_v, ub), (db_v, db)):
+                send(*pair)
+    for i, p in enumerate((p1, p2)):
+        loads[10 + i].wait()
+        send(rows_in.at[i], p)
+    for store in stores:
+        store.wait()
 
 
 def local(dp, tokens, patch_mask, mask_token, norm1_gain, norm1_shift, w_qkv, qv_bias, w_proj,
@@ -971,13 +1067,13 @@
     bits = dp.bit_length() - 1
     rows = tokens.shape[0]
     scratch = {**layer_scratch(rows), **link_scratch(bits)}
-    vmem, hbm = pl.BlockSpec(memory_space=pltpu.VMEM), pl.BlockSpec(memory_space=pl.ANY)
+    hbm = pl.BlockSpec(memory_space=pl.ANY)
     shape = jax.ShapeDtypeStruct
     out, gtok, ff, at, vec = pl.pallas_call(
         functools.partial(layer_kernel, bits, rows, INPUTS + OUTPUTS + tuple(scratch)),
         name="layer",
-        in_specs=[hbm] + [vmem] * 11 + [hbm] * 5,
-        out_specs=[hbm, hbm, hbm, hbm, vmem],
+        in_specs=[hbm] * 17,
+        out_specs=[hbm] * 5,
         out_shape=[
             shape((rows, D), BF16),
             shape((rows, D), BF16),
@@ -995,39 +1091,28 @@
         layer_scales, norm2_gain, norm2_shift, up_bias, down_bias, cotangent, w_qkv, w_proj,
         w_up, w_down,
     )
-    one = shape((D,), F32)
-    flat = pl.BlockSpec((D,), lambda j: (0,))
-    whole = pl.BlockSpec((rows, D), lambda j: (0, 0))
+    one, flat = shape((D,), F32), pltpu.VMEM((D,), F32)
     out, gtok, wu, wd, wq, wp, mt, g1, s1, qv, pb, ls, g2, s2, ub, db = pl.pallas_call(
         finish_kernel,
         name="finish",
-        grid=(6,),
-        in_specs=[
-            pl.BlockSpec((1, FF_ROWS, 128), lambda j: (j, 0, 0)),
-            pl.BlockSpec((1, AT_ROWS, 128), lambda j: (jnp.minimum(j, 3), 0, 0)),
-            pl.BlockSpec((NVEC, D), lambda j: (0, 0)),
-            whole, whole,
-        ],
-        out_specs=[
-            whole, whole,
-            pl.BlockSpec((D, 256), lambda j: (0, j)),
-            pl.BlockSpec((256, D), lambda j: (j, 0)),
-            pl.BlockSpec((3, D, 128), lambda j: (0, 0, jnp.minimum(j, 2))),
-            pl.BlockSpec((384, D), lambda j: (0, 0)),
-            flat, flat, flat,
-            pl.BlockSpec((2, 384), lambda j: (0, 0)),
-            flat,
-            pl.BlockSpec((2, D), lambda j: (0, 0)),
-            flat, flat,
-            pl.BlockSpec((2 * D,), lambda j: (0,)),
-            flat,
-        ],
+        in_specs=[hbm] * 5,
+        out_specs=[hbm] * 16,
         out_shape=[
             shape((rows, D), BF16), shape((rows, D), BF16),
             shape((D, 1536), F32), shape((1536, D), F32), shape((3, D, 384), F32),
             shape((384, D), F32), one, one, one, shape((2, 384), F32), one, shape((2, D), F32),
             one, one, shape((2 * D,), F32), one,
         ],
+        scratch_shapes=[
+            pltpu.VMEM((6, FF_ROWS, 128), BF16), pltpu.VMEM((4, AT_ROWS, 128), BF16),
+            pltpu.VMEM((NVEC, D), F32), pltpu.VMEM((2, rows, D), BF16),
+            pltpu.VMEM((6, D, 256), F32), pltpu.VMEM((6, 256, D), F32),
+            pltpu.VMEM((3, 3, D, 128), F32), pltpu.VMEM((384, D), F32),
+            flat, flat, flat, pltpu.VMEM((2, 384), F32), flat, pltpu.VMEM((2, D), F32), flat, flat,
+            pltpu.VMEM((2 * D,), F32), flat,
+            pltpu.SemaphoreType.DMA((13,)), pltpu.SemaphoreType.DMA((28,)),
+        ],
+        compiler_params=pltpu.CompilerParams(vmem_limit_bytes=62 * 2**20),
     )(ff, at, vec, out, gtok)
     return out, gtok, mt, g1, s1, wq, qv, wp, pb, ls, g2, s2, wu, ub, wd, db
 

time: 149 us -> 140 us (0.940)
  Pallas kernels: 148 us -> 139 us
    pallas_call x1, Pallas kernels: 137 us -> 130 us  [local(): pl.pallas_call(functools.partial(layer_kernel, bits, rows, INPUTS + OUTPU...]
    pallas_call x1, Pallas kernels: 10.8 us -> 8.42 us  [local(): pl.pallas_call(finish_kernel, name='finish', in_specs=[hbm] * 5, out_spec...]
where the time goes in v3:
time: 140 us; the launch traced here: 139 us
  Pallas kernels  139 us (99%)
    pallas_call x1, Pallas kernels, local(): pl.pallas_call(functools.partial(layer_kernel, bits, rows, INPUTS + OUTPU...  130 us
    pallas_call x1, Pallas kernels, local(): pl.pallas_call(finish_kernel, name='finish', in_specs=[hbm] * 5, out_spec...  8.42 us

profile of v3, /device:TPU:0, one launch (start us, length us, event | category | flops | bytes accessed | tf_op | source)
XLA Modules:
  0.0 139.4 jit_solution(17566662225636159760)
XLA Ops:
  0.7 130.2 %layer.1 = (bf16[591,768]{1,0:T(8,128)(2,1)}, bf16[591,768]{1,0:T(8,128)(2,1)}, bf16[6,3072,128]{2,1,0:T(8,128)(2,1)}, bf16[4,2304,128]{2,1,0:T(8,128)(2,1)}, f32[16,768]{1,0:T(8,128)}) custom-call(bf16[591,768]{1,0:T(8,128)(2,1)} %refs_0_.1, s32[591]{0:T(1024)} %refs_1_.1, f32[768]{0:T(1024)} %refs_2_.1, f32[768]{0:T(1024)} %refs_3_.1, f32[768]{0:T(1024)} %refs_4_.1, ...), custom_call_target="tpu_custom_call" | custom-call | flops 27000000512 | bytes 20000000 | tf_op jit(solution)/shard_map/layer/pallas_call | solution.py:1072
  130.8 8.4 %finish.1 = (bf16[591,768]{1,0:T(8,128)(2,1)}, bf16[591,768]{1,0:T(8,128)(2,1)}, f32[768,1536]{1,0:T(8,128)}, f32[1536,768]{1,0:T(8,128)}, f32[3,768,384]{2,1,0:...) custom-call(bf16[6,3072,128]{2,1,0:T(8,128)(2,1)} %get-tuple-element, ...), custom_call_target="tpu_custom_call" | custom-call | tf_op jit(solution)/shard_map/finish/pallas_call | solution.py:1095

commit v4 on v3

--- a/solution.py
+++ b/solution.py
@@ -143,10 +143,11 @@
                 sc, _ = normed(mx)
                 self.n1[to, :] = (sc * self.n1g[...] + self.n1s[...]).astype(BF16)
 
-    def start2(self):
+    def turn1(self):
         self.n1t[...] = jnp.transpose(self.n1[...])
+
+    def spread(self):
         self.io_copy(1).wait()
-        self.clear()
         self.widen(self.cot)
         for i in range(self.images):
             for r, n in BLOCKS:
@@ -174,22 +175,27 @@
         zero = jnp.zeros_like(x)
         return jnp.where(low, x, zero), jnp.where(low, zero, x)
 
+    def softmax(self, s):
+        tail = s[LP - 16 :]
+        keep = lax.broadcasted_iota(jnp.int32, tail.shape, 0) < L - (LP - 16)
+        s = jnp.concatenate([s[: LP - 16], jnp.where(keep, tail, -1e30)], axis=0)
+        x = jnp.exp(s - jnp.max(s, axis=0, keepdims=True))
+        return (x * (1.0 / jnp.sum(x, axis=0, keepdims=True))).astype(BF16)
+
     def attend(self, t):
-        for i in range(self.images):
-            at = pl.ds(i * LP, LP)
-            q0, q1 = self.two(self.q[t, at, :])
+        n = self.images
+        rows = [pl.ds(i * LP, LP) for i in range(n)]
+        scores = []
+        for at in rows:
             k = self.k[t, at, :]
+            scores.append([dot_nt(k, q) for q in self.two(self.q[t, at, :])])
+        probs = [[self.softmax(s) for s in pair] for pair in scores]
+        for i, at in enumerate(rows):
             vt = jnp.transpose(self.v[t, at, :])
             outs = []
-            for e, qe in enumerate((q0, q1)):
-                s = dot_nt(k, qe)
-                tail = s[LP - 16 :]
-                keep = lax.broadcasted_iota(jnp.int32, tail.shape, 0) < L - (LP - 16)
-                s = jnp.concatenate([s[: LP - 16], jnp.where(keep, tail, -1e30)], axis=0)
-                x = jnp.exp(s - jnp.max(s, axis=0, keepdims=True))
-                p = (x * (1.0 / jnp.sum(x, axis=0, keepdims=True))).astype(BF16)
-                self.pt[(t * self.images + i) * 2 + e] = p
-                outs.append(dot(vt[e * 64 : e * 64 + 64, :], p))
+            for e in range(2):
+                self.pt[(t * n + i) * 2 + e] = probs[i][e]
+                outs.append(dot(vt[e * 64 : e * 64 + 64, :], probs[i][e]))
             ot = jnp.concatenate(outs, axis=0).astype(BF16)
             self.hot[i, pl.ds(pl.multiple_of(t * 128, 128), 128), :] = ot
             self.ho[t, at, :] = jnp.transpose(ot)
@@ -229,16 +235,15 @@
             [self.g_ff[j, h, pl.ds(1536 + b * D, D), :] for b in range(2)], axis=1)
         row = h * 6 + j
         pre = dot(self.n2[...], wu) + self.ub[pl.ds(row, 1), :]
+        ga = dot_nt(self.gb[...], wd)
         cdf = 0.5 * (1.0 + lax.erf(pre * INV_ROOT2))
         act = (pre * cdf).astype(BF16)
-        slope = cdf + pre * jnp.exp(-0.5 * pre * pre) * INV_ROOT2PI
-        gp32 = dot_nt(self.gb[...], wd) * slope
-        gp = gp32.astype(BF16)
+        gp = (ga * (cdf + pre * jnp.exp(-0.5 * pre * pre) * INV_ROOT2PI)).astype(BF16)
+        self.br2[...] += dot(act, wd)
+        gwd = dot(jnp.transpose(act), self.gb[...]).astype(BF16)
+        self.gn2[...] += dot_nt(gp, wu)
+        gwu = dot(self.n2t[...], gp).astype(BF16)
         self.uba[row] = fold(gp.astype(F32))
-        self.br2[...] += dot(act, wd)
-        self.gn2[...] += dot_nt(gp, wu)
-        gwd = dot(jnp.transpose(act), self.gb[...]).astype(BF16)
-        gwu = dot(self.n2t[...], gp).astype(BF16)
         for b in range(6):
             self.g_ff[j, h, pl.ds(b * 256, 256), :] = gwd[:, b * 128 : b * 128 + 128]
         for b in range(2):
@@ -293,22 +298,26 @@
                 :, b * 128 : b * 128 + 128].astype(BF16)
 
     def attend_back(self, t):
-        for i in range(self.images):
-            at = pl.ds(i * LP, LP)
-            q0, q1 = self.two(self.q[t, at, :])
-            d0, d1 = self.two(self.ho[t, at, :])
-            k = self.k[t, at, :]
+        n = self.images
+        rows = [pl.ds(i * LP, LP) for i in range(n)]
+        grads = []
+        for at in rows:
             v = self.v[t, at, :]
-            kt = jnp.transpose(k)
-            dq, dk, dv = [], 0.0, 0.0
-            for e, (qe, de) in enumerate(((q0, d0), (q1, d1))):
-                pb = self.pt[(t * self.images + i) * 2 + e]
-                p = pb.astype(F32)
-                gp = dot_nt(v, de)
-                gs = (p * (gp - jnp.sum(gp * p, axis=0, keepdims=True))).astype(BF16)
-                dv = dv + dot(pb, de)
-                dk = dk + dot(gs, qe)
-                dq.append(dot(kt[e * 64 : e * 64 + 64, :], gs))
+            grads.append([dot_nt(v, d) for d in self.two(self.ho[t, at, :])])
+        scores = []
+        for i in range(n):
+            pair = []
+            for e in range(2):
+                p, gp = self.pt[(t * n + i) * 2 + e].astype(F32), grads[i][e]
+                pair.append((p * (gp - jnp.sum(gp * p, axis=0, keepdims=True))).astype(BF16))
+            scores.append(pair)
+        for i, at in enumerate(rows):
+            q, d = self.two(self.q[t, at, :]), self.two(self.ho[t, at, :])
+            kt = jnp.transpose(self.k[t, at, :])
+            gs = scores[i]
+            dv = dot(self.pt[(t * n + i) * 2], d[0]) + dot(self.pt[(t * n + i) * 2 + 1], d[1])
+            dk = dot(gs[0], q[0]) + dot(gs[1], q[1])
+            dq = [dot(kt[e * 64 : e * 64 + 64, :], gs[e]) for e in range(2)]
             dq = jnp.transpose(jnp.concatenate(dq, axis=0)) * 0.125
             self.dqkv[at, 0:128] = dq.astype(BF16)
             self.dqkv[at, 128:256] = dk.astype(BF16)
@@ -401,16 +410,16 @@
 
 Y_FIRST, Z_FIRST = (0, "y", 1, 2, 3), (0, 2, "y", 1, 3)
 CUTS = {
-    0: ((3, (0, 'y', 'F', 'M', 11), -44), (6, (0, 1, 'y', 'F', 'MM'), -11), (3, (0, 'y', 11, 'F', 'MM'), -8),),
-    1: ((1, (0, 'y', 'F', 11, 'MM'), -54), (3, (0, 'y', 'F', 'M', 11), -8), (8, (0, 1, 'y', 'F', 'MM'), -31),),
-    2: ((4, (0, 1, 'y', 'F', 'MM'), -23), (8, (0, 'y', 1, 'F', 'MM'), -27),),
-    3: ((3, (0, 'y', 11, 'F', 'MM'), 45), (4, (0, 1, 'y', 'F', 'MM'), -3), (3, (0, 'F', 'M', 'y', 11), -6), (2, (0, 'F', 'M', 'y', 11), -60),),
-    4: ((9, (0, 1, 'F', 'M', 'y'), -20), (3, (0, 'y', 1, 'F', 'MM'), -39),),
-    5: ((7, (0, 'y', 1, 'F', 'MM'), -10), (5, (0, 'y', 1, 'F', 'MM'), 28),),
-    9: ((9, (0, 'y', 1, 'F', 'MM'), -26),),
-    6: ((4, (0, 'y', 1, 'F', 'M'), -43), (5, (0, 'y', 2, 1, 13), -14),),
-    7: ((4, (0, 'y', 1, 'F', 'MM'), 35), (5, (0, 2, 'y', 1, 13), 32),),
-    8: ((2, (0, 'F', 'M', 'y', 11), 7), (5, (0, 'y', 1, 'F', 'MM'), 1), (2, (0, 'y', 1, 'F', 'MM'), -18),),
+    0: ((6, (0, 1, 'y', 'F', 'M'), -33), (6, (0, 'y', 1, 'F', 'MM'), -41),),
+    1: ((3, (0, 1, 'y', 'F', 'M'), 28), (4, (0, 3, 2, 'y', 11), -25), (2, (0, 'y', 11, 'F', 'MM'), -56), (3, (0, 'y', 'F', 'M', 11), 10),),
+    2: ((8, (0, 1, 'y', 'F', 'MM'), 46), (4, (0, 'y', 1, 'F', 'M'), -10),),
+    3: ((3, (0, 'y', 'F', 'M', 11), 33), (3, (0, 'y', 1, 'F', 'MM'), -21), (6, (0, 1, 'y', 'F', 'MM'), -20),),
+    4: ((7, (0, 2, 'y', 1, 13), -30), (5, (0, 'y', 1, 'F', 'MM'), -30),),
+    5: ((4, (0, 'y', 'F', 'M', 1), 54), (8, (0, 1, 'y', 'F', 'MM'), 31),),
+    9: ((7, (0, 'y', 1, 'F', 'M'), 55), (2, (0, 'y', 2, 3, 1), 15),),
+    6: ((1, (0, 1, 'F', 'y', 'MM'), -25), (4, (0, 'y', 1, 'F', 'MM'), 46), (4, (0, 'y', 1, 'F', 'MM'), -27),),
+    7: ((4, (0, 'y', 1, 'F', 'MM'), -1), (5, (0, 'y', 1, 'F', 'MM'), -10),),
+    8: ((1, (0, 'y', 'F', 'M', 11), 12), (3, (0, 'y', 'F', 'M', 11), 43), (3, (0, 'y', 1, 'F', 'MM'), 5), (2, (0, 'y', 1, 'F', 'M'), 20),),
 }
 
 
@@ -724,8 +733,8 @@
     )
 
 
-ROUTES = ((('y', 1, 2), ('y', 2)), (('y', 1, 2), ('y', 2)), (('y', 1, 2), ('y', 1)), (('y', 2, 1), ('y', 1, 2)), (('y', 1, 2), ('y', 2)), (('y',), ('y', 2)), (('y', 2, 1), ('y', 1, 2)), (('y', 2), ('y', 2, 1)), (('y', 1, 2), ('y', 1)), (('y', 2), ('y', 2, 1)))
-GATHER_ORDER = (6, 7, 8, 9, 0, 1, 2, 3, 4, 5)
+ROUTES = ((('y', 1, 2), ('y', 1)), (('y', 2), ('y', 1, 2)), (('y', 2, 1), ('y', 1)), (('y', 1, 2), ('y', 2)), (('y', 2), ('y', 1, 2)), (('y', 2), ('y', 2)), (('y', 1, 2), ('y', 2, 1)), (('y', 1, 2), ('y', 1)), (('y', 1, 2), ('y', 1, 2)), (('y', 1), ('y', 2)))
+GATHER_ORDER = (8, 6, 7, 9, 0, 1, 2, 3, 4, 5)
 
 
 def gather_plan(k, sub):
@@ -736,10 +745,10 @@
     return steps + [(0, rows)]
 
 
-SLACK, STEP, BACKLOG = 0.2, 0.05, 2.372
+SLACK, STEP, BACKLOG = 0.2, 0.05, 4.338
 HOPS = {0: 0.9, "y": 2.2, 1: 2.2, 2: 2.2, "F": 2.2, "U": 2.2, "M": 2.2}
 FAR_HOP = 2.7
-LINK, CORES, SUMS, MESSAGE, LOADS, ENTRY = 45.5e3, 480e3, 2.4e6, 0.1, 3.0e6, 3.8
+LINK, CORES, SUMS, MESSAGE, LOADS, ENTRY = 46.0e3, 480e3, 2.4e6, 0.09, 3.0e6, 3.8
 LINES = {
     0: (("c", 1),), "y": (("y", 1),), 1: (("x", 1),), 2: (("zi", 1), ("zo", 1)), "F": (("zi", 1),),
     "U": (("zo", 1),), "M": (("mid", 1),), "MM": (("mid", 1),)}
@@ -748,15 +757,15 @@
 
 def compute_pieces():
     out = [("start", 0.5, None)]
-    out += [(("qa", t, s), (0.57, 1.45)[s], None) for t in range(3) for s in range(2)]
-    out += [("start2", 1.7, None)]
-    out += [(("qa", t, s), (0.57, 1.45)[s], 3 + t if s == 0 else None)
+    out += [(("qa", t, s), (0.57, 0.8)[s], None) for t in range(3) for s in range(2)]
+    out += [("spread", 0.9, None), ("clear", 0.4, None), ("turn1", 0.4, None)]
+    out += [(("qa", t, s), (0.57, 0.8)[s], 3 + t if s == 0 else None)
             for t in range(3, 6) for s in range(2)]
-    out += [("project", 1.6, 9), ("second_norm", 0.8, None), ("turn", 0.6, None)]
-    out += [(("feed", u, 0), 1.96, u // 2 if u % 2 == 0 else None) for u in range(12)]
-    out += [(("middle_back", i, 0), 1.2, None) for i in range(3)]
-    out += [("proj_back", 1.0, None), ("proj_grad", 1.6, None)]
-    out += [(("back", u, s), (1.62, 1.4)[s], None) for u in range(6) for s in range(2)]
+    out += [("project", 1.2, 9), ("second_norm", 0.8, None), ("turn", 0.5, None)]
+    out += [(("feed", u, 0), 1.88, u // 2 if u % 2 == 0 else None) for u in range(12)]
+    out += [(("middle_back", i, 0), 1.33, None) for i in range(3)]
+    out += [("proj_back", 1.0, None), ("proj_grad", 1.5, None)]
+    out += [(("back", u, s), (0.9, 1.25)[s], None) for u in range(6) for s in range(2)]
     out += [(("first_back", i, 0), 0.8, None) for i in range(3)]
     out += [("sums", 0.6, None), ("output", 0.6, None), ("tokens", 0.6, None)]
     after = {("feed", 2 * j + 1, 0): j for j in range(6)}
@@ -820,7 +829,7 @@
             del self.tasks[key]
             if key[0] == "l":
                 for sub in range(2):
-                    self.tasks["w", key[1], sub] = (0, self.now)
+                    self.tasks["w", key[1], sub] = (0, self.now - SLACK)
             return
         way, nbytes = self.moves[key][stage]
         lines = LINES.get(way, FAR_LINES)
@@ -843,10 +852,10 @@
         self.poll(0.0)
 
     def run(self):
-        loaded = ENTRY
+        loaded = 0.0
         for k in GATHER_ORDER:
             loaded += CHUNKS[k][2] * 256 / LOADS
-            self.tasks["l", k] = (0, loaded)
+            self.tasks["l", k] = (0, max(ENTRY, 2.5 + loaded) - SLACK)
         pieces, after = compute_pieces()
         for piece, took, needs in pieces:
             self.poll(SLACK)
@@ -929,7 +938,9 @@
 
     single = {
         "start": y.start,
-        "start2": y.start2,
+        "spread": y.spread,
+        "clear": y.clear,
+        "turn1": y.turn1,
         "project": y.project,
         "second_norm": y.second_norm,
         "turn": y.turn,

time: 140 us -> 137 us (0.979)
  Pallas kernels: 139 us -> 137 us
    pallas_call x1, Pallas kernels: 130 us -> 128 us  [local(): pl.pallas_call(functools.partial(layer_kernel, bits, rows, INPUTS + OUTPU...]
where the time goes in v4:
time: 137 us
  Pallas kernels  137 us (100%)
    pallas_call x1, Pallas kernels, local(): pl.pallas_call(functools.partial(layer_kernel, bits, rows, INPUTS + OUTPU...  128 us
    pallas_call x1, Pallas kernels, local(): pl.pallas_call(finish_kernel, name='finish', in_specs=[hbm] * 5, out_spec...  8.42 us

profile of v4, /device:TPU:0, one launch (start us, length us, event | category | flops | bytes accessed | tf_op | source)
XLA Modules:
  0.0 137.3 jit_solution(15051187812805183319)
XLA Ops:
  0.7 128.1 %layer.1 = (bf16[591,768]{1,0:T(8,128)(2,1)}, bf16[591,768]{1,0:T(8,128)(2,1)}, bf16[6,3072,128]{2,1,0:T(8,128)(2,1)}, bf16[4,2304,128]{2,1,0:T(8,128)(2,1)}, f32[16,768]{1,0:T(8,128)}) custom-call(bf16[591,768]{1,0:T(8,128)(2,1)} %refs_0_.1, s32[591]{0:T(1024)} %refs_1_.1, f32[768]{0:T(1024)} %refs_2_.1, f32[768]{0:T(1024)} %refs_3_.1, f32[768]{0:T(1024)} %refs_4_.1, ...), custom_call_target="tpu_custom_call" | custom-call | flops 27000000512 | bytes 20000000 | tf_op jit(solution)/shard_map/layer/pallas_call | solution.py:1083
  128.8 8.4 %finish.1 = (bf16[591,768]{1,0:T(8,128)(2,1)}, bf16[591,768]{1,0:T(8,128)(2,1)}, f32[768,1536]{1,0:T(8,128)}, f32[1536,768]{1,0:T(8,128)}, f32[3,768,384]{2,1,0:...) custom-call(bf16[6,3072,128]{2,1,0:T(8,128)(2,1)} %get-tuple-element, ...), custom_call_target="tpu_custom_call" | custom-call | tf_op jit(solution)/shard_map/finish/pallas_call | solution.py:1106

commit v5 on v4

--- a/solution.py
+++ b/solution.py
@@ -410,16 +410,16 @@
 
 Y_FIRST, Z_FIRST = (0, "y", 1, 2, 3), (0, 2, "y", 1, 3)
 CUTS = {
-    0: ((6, (0, 1, 'y', 'F', 'M'), -33), (6, (0, 'y', 1, 'F', 'MM'), -41),),
-    1: ((3, (0, 1, 'y', 'F', 'M'), 28), (4, (0, 3, 2, 'y', 11), -25), (2, (0, 'y', 11, 'F', 'MM'), -56), (3, (0, 'y', 'F', 'M', 11), 10),),
-    2: ((8, (0, 1, 'y', 'F', 'MM'), 46), (4, (0, 'y', 1, 'F', 'M'), -10),),
-    3: ((3, (0, 'y', 'F', 'M', 11), 33), (3, (0, 'y', 1, 'F', 'MM'), -21), (6, (0, 1, 'y', 'F', 'MM'), -20),),
-    4: ((7, (0, 2, 'y', 1, 13), -30), (5, (0, 'y', 1, 'F', 'MM'), -30),),
-    5: ((4, (0, 'y', 'F', 'M', 1), 54), (8, (0, 1, 'y', 'F', 'MM'), 31),),
-    9: ((7, (0, 'y', 1, 'F', 'M'), 55), (2, (0, 'y', 2, 3, 1), 15),),
-    6: ((1, (0, 1, 'F', 'y', 'MM'), -25), (4, (0, 'y', 1, 'F', 'MM'), 46), (4, (0, 'y', 1, 'F', 'MM'), -27),),
-    7: ((4, (0, 'y', 1, 'F', 'MM'), -1), (5, (0, 'y', 1, 'F', 'MM'), -10),),
-    8: ((1, (0, 'y', 'F', 'M', 11), 12), (3, (0, 'y', 'F', 'M', 11), 43), (3, (0, 'y', 1, 'F', 'MM'), 5), (2, (0, 'y', 1, 'F', 'M'), 20),),
+    0: ((5, (0, 'y', 'F', 'M', 11), 49), (7, (0, 1, 'y', 'F', 'MM'), 2),),
+    1: ((3, (0, 'y', 11, 'F', 'MM'), -58), (5, (0, 'y', 2, 1, 13), 58), (4, (0, 1, 'y', 'F', 'MM'), -28),),
+    2: ((4, (0, 'y', 1, 'F', 'MM'), -60), (8, (0, 1, 'y', 'F', 'MM'), -33),),
+    3: ((8, (0, 2, 'y', 1, 13), 40), (4, (0, 'y', 'F', 'M', 11), -60),),
+    4: ((3, (0, 1, 'F', 'MM', 'y'), -7), (9, (0, 'y', 1, 'F', 'MM'), -13),),
+    5: ((3, (0, 1, 'y', 'F', 'MM'), 26), (7, (0, 1, 'y', 'F', 'MM'), -37), (2, (0, 'y', 2, 11, 13), -46),),
+    9: ((9, (0, 'y', 1, 'F', 'MM'), -5),),
+    6: ((3, (0, 1, 'F', 'M', 'y'), -25), (6, (0, 'y', 1, 'F', 'MM'), 37),),
+    7: ((1, (0, 'F', 'M', 'y', 1), -40), (1, (0, 'y', 'F', 'M', 11), 21), (4, (0, 'y', 'F', 'M', 11), -2), (3, (0, 'y', 1, 'F', 'MM'), 17),),
+    8: ((1, (0, 'y', 1, 'F', 'M'), -29), (3, (0, 'y', 1, 'F', 'MM'), -60), (2, (0, 'y', 1, 'F', 'MM'), 38), (1, (0, 'y', 1, 'F', 'MM'), 3), (2, (0, 'y', 1, 'F', 'MM'), 1),),
 }
 
 
@@ -577,8 +577,7 @@
         def _(b):
             to = pl.ds(pl.multiple_of(dst_at + b * size, 16), size)
             of = pl.ds(pl.multiple_of(src_at + b * size, 16), size)
-            total = dst[to, :].astype(F32) + src[of, :].astype(F32)
-            dst[to, :] = total.astype(BF16)
+            dst[to, :] = dst[to, :] + src[of, :]
 
     def when(self, role):
         if role == "all":
@@ -733,8 +732,8 @@
     )
 
 
-ROUTES = ((('y', 1, 2), ('y', 1)), (('y', 2), ('y', 1, 2)), (('y', 2, 1), ('y', 1)), (('y', 1, 2), ('y', 2)), (('y', 2), ('y', 1, 2)), (('y', 2), ('y', 2)), (('y', 1, 2), ('y', 2, 1)), (('y', 1, 2), ('y', 1)), (('y', 1, 2), ('y', 1, 2)), (('y', 1), ('y', 2)))
-GATHER_ORDER = (8, 6, 7, 9, 0, 1, 2, 3, 4, 5)
+ROUTES = ((('y', 1, 2), ('y', 2, 1)), (('y', 2, 1), ('y', 1, 2)), (('y', 2), ('y', 2)), (('y', 1, 2), ('y', 2)), (('y', 2), ('y',)), (('y', 2), ('y', 2)), (('y', 2, 1), ('y', 1, 2)), (('y', 2, 1), ('y', 1, 2)), (('y', 1, 2), ('y', 1)), (('y', 1), ('y', 2)))
+GATHER_ORDER = (6, 7, 8, 0, 9, 1, 2, 3, 4, 5)
 
 
 def gather_plan(k, sub):
@@ -745,10 +744,10 @@
     return steps + [(0, rows)]
 
 
-SLACK, STEP, BACKLOG = 0.2, 0.05, 4.338
+SLACK, STEP, BACKLOG = 0.2, 0.08, 2.417
 HOPS = {0: 0.9, "y": 2.2, 1: 2.2, 2: 2.2, "F": 2.2, "U": 2.2, "M": 2.2}
 FAR_HOP = 2.7
-LINK, CORES, SUMS, MESSAGE, LOADS, ENTRY = 46.0e3, 480e3, 2.4e6, 0.09, 3.0e6, 3.8
+LINK, CORES, SUMS, MESSAGE, LOADS, ENTRY = 47.0e3, 480e3, 2.4e6, 0.01, 3.0e6, 3.8
 LINES = {
     0: (("c", 1),), "y": (("y", 1),), 1: (("x", 1),), 2: (("zi", 1), ("zo", 1)), "F": (("zi", 1),),
     "U": (("zo", 1),), "M": (("mid", 1),), "MM": (("mid", 1),)}

time: 137 us -> 136 us (level)
  Pallas kernels: 137 us -> 135 us
    pallas_call x1, Pallas kernels: 128 us -> 127 us  [local(): pl.pallas_call(functools.partial(layer_kernel, bits, rows, INPUTS + OUTPU...]
where the time goes in v5:
time: 136 us
  Pallas kernels  135 us (99%)
    pallas_call x1, Pallas kernels, local(): pl.pallas_call(functools.partial(layer_kernel, bits, rows, INPUTS + OUTPU...  127 us
    pallas_call x1, Pallas kernels, local(): pl.pallas_call(finish_kernel, name='finish', in_specs=[hbm] * 5, out_spec...  8.42 us

profile of v5, /device:TPU:0, one launch (start us, length us, event | category | flops | bytes accessed | tf_op | source)
XLA Modules:
  0.0 135.8 jit_solution(16622139661956157955)
XLA Ops:
  0.7 126.5 %layer.1 = (bf16[591,768]{1,0:T(8,128)(2,1)}, bf16[591,768]{1,0:T(8,128)(2,1)}, bf16[6,3072,128]{2,1,0:T(8,128)(2,1)}, bf16[4,2304,128]{2,1,0:T(8,128)(2,1)}, f32[16,768]{1,0:T(8,128)}) custom-call(bf16[591,768]{1,0:T(8,128)(2,1)} %refs_0_.1, s32[591]{0:T(1024)} %refs_1_.1, f32[768]{0:T(1024)} %refs_2_.1, f32[768]{0:T(1024)} %refs_3_.1, f32[768]{0:T(1024)} %refs_4_.1, ...), custom_call_target="tpu_custom_call" | custom-call | flops 27000000512 | bytes 20000000 | tf_op jit(solution)/shard_map/layer/pallas_call | solution.py:1082
  127.2 8.4 %finish.1 = (bf16[591,768]{1,0:T(8,128)(2,1)}, bf16[591,768]{1,0:T(8,128)(2,1)}, f32[768,1536]{1,0:T(8,128)}, f32[1536,768]{1,0:T(8,128)}, f32[3,768,384]{2,1,0:...) custom-call(bf16[6,3072,128]{2,1,0:T(8,128)(2,1)} %get-tuple-element, ...), custom_call_target="tpu_custom_call" | custom-call | tf_op jit(solution)/shard_map/finish/pallas_call | solution.py:1105
